TPU v7x, 1024 devices: a whole 4x8x16 slice. The times are simulated.
1024 devices in a mesh: group: 16 (over z), expert: 64 (over x, y, core).
Axes of the slice: x: 4, y: 8, z: 16, core: 2. Of those that a mesh axis runs over, the one named last changes fastest.
Arguments:
- grad_out: bfloat16 [64, 48, 4096], P('expert', 'group'), may hold values from -2 to 2
- inputs: bfloat16 [64, 48, 4096], P('expert', 'group'), may hold values from -6 to 6
- expert_ids: int32 [64, 48, 8], P('expert'), may hold values from 0 to 127, all different within a row; in each aligned block of 48 rows (0 to 47, 48 to 95, ..., all dimensions but the last counted through in order) at most 4 rows name the same one
- route_weights: float32 [64, 48, 8], P('expert'), may hold values from 0.05 to 1
- w_gate: bfloat16 [1024, 512, 1024], P(('group', 'expert')), may hold values from -0.09375 to 0.09375
- w_up: bfloat16 [1024, 512, 1024], P(('group', 'expert')), may hold values from -0.09375 to 0.09375
- w_down: bfloat16 [1024, 1024, 512], P(('group', 'expert')), may hold values from -0.1875 to 0.1875
Outputs:
- grad_in: float32 [64, 48, 4096], P('expert', 'group')
- grad_route: float32 [64, 48, 8], P('expert', 'group')
Inputs may be any that keep to these rules, and one draw needn't show every extreme that they name: `expert_ids`: each token names 8 different experts; expert e belongs to group e // 8. Among the 48 tokens of one index of the expert axis (one aligned block of the leading dimensions) no expert is named more than 4 times, a bound that some block reaches.
All inputs are finite; a program needn't handle non-finite values.
Results may differ from a plain program's by a relative error of at most 0.0029.
Values may be sent and summed in bfloat16 or wider, within the bound.
No kernel may reach another device: no remote copies, remote signals or barrier semaphores. Data moves between devices by JAX's collectives and lax.ppermute only.
A program may use at most 32 MiB of HBM per device.

v0:
```python
import jax
import jax.numpy as jnp
from jax import lax
from jax.sharding import PartitionSpec as P


def from_partner(value, axis, bit):
    mask = 2**bit
    pairs = [(source, source ^ mask) for source in range(lax.axis_size(axis))]
    return lax.ppermute(value, axis, pairs)


def silu_slope(value):
    sig = jax.nn.sigmoid(value)
    return sig * (1.0 + value * (1.0 - sig))


def body(grad_out, inputs, expert_ids, route_weights, w_gate, w_up, w_down):
    groups = lax.axis_size("group")
    members = lax.axis_size("expert")
    slices = min(8, members // 4)
    exp_grp = members // slices
    depth_count = slices.bit_length() - 1
    member = lax.axis_index("expert")
    group_id = lax.axis_index("group")
    tok_dev = grad_out.shape[1]
    model_width = grad_out.shape[2]
    part_width = w_gate.shape[1]
    hidden = w_gate.shape[2]
    block_width = hidden // slices
    routes = expert_ids[0]
    weights = route_weights[0]
    column = routes.shape[0]
    top_count = routes.shape[1]
    most = max(2, 3 * column * top_count // (2 * exp_grp * groups))
    row_count = members * most
    route_groups = routes // exp_grp
    own_groups = lax.dynamic_slice_in_dim(route_groups, group_id * tok_dev, tok_dev, 0)
    group_range = jnp.arange(groups, dtype=jnp.int32)
    target = jnp.any(own_groups[None, :, :] == group_range[:, None, None], axis=2)
    zero_value = jnp.zeros((), jnp.bfloat16)
    send_grad = jnp.where(target[:, :, None], grad_out[0][None], zero_value)
    send_input = jnp.where(target[:, :, None], inputs[0][None], zero_value)
    got_grad, got_input = (
        lax.all_to_all(send_grad, "group", split_axis=0, concat_axis=0, tiled=True),
        lax.all_to_all(send_input, "group", split_axis=0, concat_axis=0, tiled=True),
    )
    column_grad = got_grad.reshape(column, slices, part_width)
    column_input = got_input.reshape(column, slices, part_width)
    local_ids = group_id * exp_grp + jnp.arange(exp_grp, dtype=jnp.int32)
    matches = (routes[:, :, None] == local_ids[None, None, :]).astype(jnp.int32)
    ranking = (
        jnp.cumsum(matches.reshape(column * top_count, exp_grp), axis=0).reshape(
            column, top_count, exp_grp
        )
        - 1
    )
    slot_range = jnp.arange(most, dtype=jnp.int32)
    slot_pick = ((matches[..., None] == 1) & (ranking[..., None] == slot_range)).astype(jnp.float32)
    select = jnp.sum(slot_pick, axis=1).astype(jnp.bfloat16)
    pack_grad = jnp.einsum("cem,cqd->eqmd", select, column_grad, preferred_element_type=jnp.float32)
    pack_input = jnp.einsum(
        "cem,cqd->eqmd", select, column_input, preferred_element_type=jnp.float32
    )
    pack_grad = pack_grad.astype(jnp.bfloat16).reshape(members, most, part_width)
    pack_input = pack_input.astype(jnp.bfloat16).reshape(members, most, part_width)
    held_grad, held_input = (
        lax.all_to_all(pack_grad, "expert", split_axis=0, concat_axis=0, tiled=True),
        lax.all_to_all(pack_input, "expert", split_axis=0, concat_axis=0, tiled=True),
    )
    held_grad = held_grad.reshape(row_count, part_width)
    held_input = held_input.reshape(row_count, part_width)
    gate_weight = w_gate[0]
    up_weight = w_up[0]
    contract = (((1,), (1,)), ((), ()))
    gate_part = jnp.dot(held_input, gate_weight, preferred_element_type=jnp.float32)
    up_part = jnp.dot(held_input, up_weight, preferred_element_type=jnp.float32)
    down_part = lax.dot_general(held_grad, w_down[0], contract, preferred_element_type=jnp.float32)
    partials = jnp.stack([gate_part, up_part, down_part], axis=1).reshape(
        row_count, 3, slices, block_width
    )
    for depth_level in reversed(range(depth_count)):
        own_bit = member // (1 << depth_level) % 2
        halves = partials.reshape(row_count, 3, 2, -1, block_width)
        kept = lax.dynamic_index_in_dim(halves, own_bit, 2, keepdims=False)
        partner = lax.dynamic_index_in_dim(halves, 1 - own_bit, 2, keepdims=False)
        partials = kept + from_partner(partner, "expert", depth_level)
    shares = partials.reshape(row_count, 3, block_width)
    gate_sum = shares[:, 0]
    up_sum = shares[:, 1]
    down_sum = shares[:, 2]
    hidden_val = jax.nn.silu(gate_sum) * up_sum
    route_part = jnp.sum(hidden_val * down_sum, axis=1)
    gathered = shares
    for depth_level in range(depth_count):
        own_bit = member // (1 << depth_level) % 2
        partner = from_partner(gathered, "expert", depth_level)
        gathered = jnp.where(
            own_bit == 0,
            jnp.concatenate([gathered, partner], axis=2),
            jnp.concatenate([partner, gathered], axis=2),
        )
    full_gate = gathered[:, 0]
    full_up = gathered[:, 1]
    full_down = gathered[:, 2]
    grad_gate = (full_down * full_up * silu_slope(full_gate)).astype(jnp.bfloat16)
    grad_up = (full_down * jax.nn.silu(full_gate)).astype(jnp.bfloat16)
    returned = lax.dot_general(grad_gate, gate_weight, contract, preferred_element_type=jnp.float32)
    returned = returned + lax.dot_general(
        grad_up, up_weight, contract, preferred_element_type=jnp.float32
    )
    back_grad, back_route = (
        lax.all_to_all(
            returned.reshape(members, most, part_width),
            "expert",
            split_axis=0,
            concat_axis=0,
            tiled=True,
        ),
        lax.all_to_all(
            route_part.reshape(members, most), "expert", split_axis=0, concat_axis=0, tiled=True
        ),
    )
    weighted = jnp.sum(slot_pick * weights[:, :, None, None], axis=1)
    token_grad = jnp.einsum(
        "cem,esmd->csd",
        weighted,
        back_grad.reshape(exp_grp, slices, most, part_width),
        precision=lax.Precision.HIGHEST,
    )
    token_grad = token_grad.reshape(groups, tok_dev, model_width)
    route_sum = jnp.sum(back_route.reshape(exp_grp, slices, most), axis=1)
    token_route = jnp.einsum("ckem,em->ck", slot_pick, route_sum, precision=lax.Precision.HIGHEST)
    token_route = token_route.reshape(groups, tok_dev, top_count)
    home_grad, home_route = (
        lax.all_to_all(token_grad, "group", split_axis=0, concat_axis=0, tiled=True),
        lax.all_to_all(token_route, "group", split_axis=0, concat_axis=0, tiled=True),
    )
    return (jnp.sum(home_grad, axis=0)[None], jnp.sum(home_route, axis=0)[None])


def solution(mesh):
    placed = (
        P("expert", "group", None),
        P("expert", "group", None),
        P("expert", None, None),
        P("expert", None, None),
        P(("group", "expert"), None, None),
        P(("group", "expert"), None, None),
        P(("group", "expert"), None, None),
    )
    return jax.shard_map(
        body,
        mesh=mesh,
        in_specs=placed,
        out_specs=(P("expert", "group", None), P("expert", "group", None)),
        check_vma=False,
    )
```

profile of v0, /device:TPU:6, one launch (start us, length us, event | category | flops | bytes accessed | tf_op | source)
XLA Modules:
  0.0 433.2 jit_solution(11045372114156072982)
XLA Ops:
  0.7 0.8 add_select_fusion
  1.8 2.0 broadcast_select_fusion.1
  3.8 47.7 %all_to_all.44 = bf16[16,3,4096]{2,1,0:T(4,128)(2,1)S(1)} all-to-all(bf16[16,3,4096]{2,1,0:T(4,128)(2,1)S(1)} %get-tuple-element.18), channel_id=1, replica_groups=mesh['group'=16,'expert'=64] {'group'}, dimensions={0} | all-to-all | bytes 786432 | tf_op jit(solution)/shard_map/all_to_all | solution.py:46
  51.5 6.3 %all-to-all-start.2 = ((bf16[16,3,4096]{2,1,0:T(4,128)(2,1)}), bf16[16,3,4096]{2,1,0:T(4,128)(2,1)S(1)}, u32[]{:S(2)}, u32[]{:S(2)}) async-start(bf16[16,3,4096]{2,1,0:T(4,128)(2,1)} %get-tuple-element.19), calls=%async_computation.2 | async-start | bytes 1048576 | tf_op jit(solution)/shard_map/all_to_all | solution.py:45
  58.1 0.8 reduce-window.6
  58.9 0.2 slice_reduce_fusion
  59.7 0.5 reshape.133
  60.2 0.2 fusion
  60.6 0.9 copy.121
  61.5 25.4 %all-to-all-done.2 = bf16[16,3,4096]{2,1,0:T(4,128)(2,1)S(1)} async-done(((bf16[16,3,4096]{2,1,0:T(4,128)(2,1)}), bf16[16,3,4096]{2,1,0:T(4,128)(2,1)S(1)}, u32[]{:S(2)}, u32[]{:S(2)}) %all-to-all-start.2) | async-done | bytes 393248 | tf_op jit(solution)/shard_map/all_to_all | solution.py:45
  86.9 10.8 %all-to-all-start.1 = ((bf16[64,4,512]{2,1,0:T(4,128)(2,1)}), bf16[64,4,512]{2,1,0:T(4,128)(2,1)S(1)}, u32[]{:S(2)}, u32[]{:S(2)}) async-start(bf16[64,4,512]{2,1,0:T(4,128)(2,1)} %copy.121), calls=%async_computation.1 | async-start | bytes 524288 | tf_op jit(solution)/shard_map/all_to_all | solution.py:69
  97.8 0.5 reshape.138
  98.3 0.2 fusion.1
  98.7 0.9 copy.126
  99.6 9.7 %all-to-all-done.1 = bf16[64,4,512]{2,1,0:T(4,128)(2,1)S(1)} async-done(((bf16[64,4,512]{2,1,0:T(4,128)(2,1)}), bf16[64,4,512]{2,1,0:T(4,128)(2,1)S(1)}, u32[]{:S(2)}, u32[]{:S(2)}) %all-to-all-start.1) | async-done | bytes 262176 | tf_op jit(solution)/shard_map/all_to_all | solution.py:69
  109.3 6.7 %all-to-all-start.3 = ((bf16[64,4,512]{2,1,0:T(4,128)(2,1)}), bf16[64,4,512]{2,1,0:T(4,128)(2,1)}, u32[]{:S(2)}, u32[]{:S(2)}) async-start(bf16[64,4,512]{2,1,0:T(4,128)(2,1)} %copy.126), calls=%async_computation.3 | async-start | bytes 524288 | tf_op jit(solution)/shard_map/all_to_all | solution.py:68
  116.0 1.5 copy.150
  117.5 1.5 copy.149
  119.0 1.0 reshape.149
  120.1 1.5 convolution_bitcast_fusion.2
  121.5 1.5 convolution_bitcast_fusion.3
  123.0 4.4 %all-to-all-done.3 = bf16[64,4,512]{2,1,0:T(4,128)(2,1)} async-done(((bf16[64,4,512]{2,1,0:T(4,128)(2,1)}), bf16[64,4,512]{2,1,0:T(4,128)(2,1)}, u32[]{:S(2)}, u32[]{:S(2)}) %all-to-all-start.3) | async-done | bytes 262176 | tf_op jit(solution)/shard_map/all_to_all | solution.py:68
  127.5 1.0 reshape.151
  128.5 0.5 convolution_bitcast_fusion.1
  129.0 0.3 pad_maximum_fusion
  129.3 1.7 copy-done.1
  131.0 0.2 dynamic-slice_bitcast_fusion
  131.1 2.6 collective-permute-start
  133.8 70.4 %collective-permute-done = f32[256,3,4,128]{0,3,2,1:T(8,128)} collective-permute-done((f32[256,3,4,128]{0,3,2,1:T(8,128)S(1)}, f32[256,3,4,128]{0,3,2,1:T(8,128)}, u32[]{:S(2)}, u32[]{:S(2)}) %collective-permute-start) | collective-permute-done | bytes 1572896 | tf_op jit(solution)/shard_map/ppermute | solution.py:10
  204.2 2.1 bitcast_add_fusion
  206.4 1.9 collective-permute-start.1
  208.4 19.3 %collective-permute-done.1 = f32[256,3,2,128]{0,3,2,1:T(8,128)} collective-permute-done((f32[256,3,2,128]{0,3,2,1:T(8,128)S(1)}, f32[256,3,2,128]{0,3,2,1:T(8,128)}, u32[]{:S(2)}, u32[]{:S(2)}) %collective-permute-start.1) | collective-permute-done | bytes 786464 | tf_op jit(solution)/shard_map/ppermute | solution.py:10
  227.7 1.2 bitcast_add_fusion.1
  229.0 1.9 collective-permute-start.2
  230.9 1.7 collective-permute-done.2
  232.6 2.0 collective-permute-start.3
  234.7 1.6 collective-permute-done.3
  236.3 2.2 collective-permute-start.4
  238.6 19.4 %collective-permute-done.4 = f32[256,3,256]{0,2,1:T(8,128)} collective-permute-done((f32[256,3,256]{0,2,1:T(8,128)S(1)}, f32[256,3,256]{0,2,1:T(8,128)}, u32[]{:S(2)}, u32[]{:S(2)}) %collective-permute-start.4) | collective-permute-done | bytes 786464 | tf_op jit(solution)/shard_map/ppermute | solution.py:10
  257.9 2.1 maximum_select_fusion.1
  260.0 1.9 collective-permute-start.5
  262.0 0.7 all_to_all.33
  262.7 7.6 %all-to-all-start.6 = ((f32[64,1,4]{2,1,0:T(1,128)}), f32[64,1,4]{2,1,0:T(1,128)S(1)}, u32[]{:S(2)}, u32[]{:S(2)}) async-start(f32[64,1,4]{2,1,0:T(1,128)} %bitcast.45), calls=%async_computation.6 | async-start | bytes 65536 | tf_op jit(solution)/shard_map/all_to_all | solution.py:120
  270.4 62.1 %collective-permute-done.5 = f32[256,3,512]{0,2,1:T(8,128)} collective-permute-done((f32[256,3,512]{0,2,1:T(8,128)S(1)}, f32[256,3,512]{0,2,1:T(8,128)}, u32[]{:S(2)}, u32[]{:S(2)}) %collective-permute-start.5) | collective-permute-done | bytes 1572896 | tf_op jit(solution)/shard_map/ppermute | solution.py:10
  332.5 2.3 maximum_select_fusion
  334.8 0.7 fusion.5
  335.6 0.5 copy-done.6
  336.0 0.5 convolution_add_fusion
  336.6 0.9 reshape.144
  337.5 6.2 %all-to-all-start.4 = ((f32[64,4,512]{2,1,0:T(4,128)}), f32[64,4,512]{2,1,0:T(4,128)S(1)}, u32[]{:S(2)}, u32[]{:S(2)}) async-start(f32[64,4,512]{2,1,0:T(4,128)} %reshape.144), calls=%async_computation.4 | async-start | bytes 1048576 | tf_op jit(solution)/shard_map/all_to_all | solution.py:113
  343.7 0.2 sub.53
  344.4 0.2 select_reduce_fusion
  344.5 0.7 copy.146
  345.2 15.1 %all-to-all-done.4 = f32[64,4,512]{2,1,0:T(4,128)S(1)} async-done(((f32[64,4,512]{2,1,0:T(4,128)}), f32[64,4,512]{2,1,0:T(4,128)S(1)}, u32[]{:S(2)}, u32[]{:S(2)}) %all-to-all-start.4) | async-done | bytes 524320 | tf_op jit(solution)/shard_map/all_to_all | solution.py:113
  360.4 6.3 %all-to-all-start.7 = ((f32[16,3,8]{2,1,0:T(4,128)}), f32[16,3,8]{2,1,0:T(4,128)S(1)}, u32[]{:S(2)}, u32[]{:S(2)}) async-start(f32[16,3,8]{2,1,0:T(4,128)} %copy.146), calls=%async_computation.7 | async-start | bytes 65536 | tf_op jit(solution)/shard_map/all_to_all | solution.py:137
  366.7 0.3 copy.127
  367.0 1.1 convolution_bitcast_fusion
  368.2 1.5 copy.129
  369.7 9.7 %all-to-all-done.7 = f32[16,3,8]{2,1,0:T(4,128)S(1)} async-done(((f32[16,3,8]{2,1,0:T(4,128)}), f32[16,3,8]{2,1,0:T(4,128)S(1)}, u32[]{:S(2)}, u32[]{:S(2)}) %all-to-all-start.7) | async-done | bytes 1568 | tf_op jit(solution)/shard_map/all_to_all | solution.py:137
  379.3 3.7 all-to-all-start.5
  383.0 0.6 copy.135
  383.6 48.8 %all-to-all-done.5 = f32[16,3,4096]{2,1,0:T(4,128)S(1)} async-done(((f32[16,3,4096]{2,1,0:T(4,128)}), f32[16,3,4096]{2,1,0:T(4,128)S(1)}, u32[]{:S(2)}, u32[]{:S(2)}) %all-to-all-start.5) | async-done | bytes 786464 | tf_op jit(solution)/shard_map/all_to_all | solution.py:136
  432.4 0.2 reduce_sum.56
  432.5 0.7 broadcast_in_dim.53
  (48 shorter events, 2.3 us)
Async XLA Ops:
  0.6 127.8 %copy-start = (bf16[1,1024,512]{2,1,0:T(8,128)(2,1)S(1)}, bf16[1,1024,512]{2,1,0:T(8,128)(2,1)}, u32[]{:S(2)}) copy-start(bf16[1,1024,512]{2,1,0:T(8,128)(2,1)} %param.13) | copy-start | bytes 3145732
  0.6 57.2 %copy-start.8 = (s32[1,48,8]{1,2,0:T(8,128)S(1)}, s32[1,48,8]{1,2,0:T(8,128)}, u32[]{:S(2)}) copy-start(s32[1,48,8]{1,2,0:T(8,128)} %param.9) | copy-start | bytes 4612
  0.7 58.9 %copy-start.9 = (f32[1,48,8]{1,2,0:T(8,128)S(1)}, f32[1,48,8]{1,2,0:T(8,128)}, u32[]{:S(2)}) copy-start(f32[1,48,8]{1,2,0:T(8,128)} %param.10) | copy-start | bytes 4612
  51.5 35.4 %all-to-all-start.2 = ((bf16[16,3,4096]{2,1,0:T(4,128)(2,1)}), bf16[16,3,4096]{2,1,0:T(4,128)(2,1)S(1)}, u32[]{:S(2)}, u32[]{:S(2)}) async-start(bf16[16,3,4096]{2,1,0:T(4,128)(2,1)} %get-tuple-element.19), calls=%async_computation.2 | async-start | bytes 1048576 | tf_op jit(solution)/shard_map/all_to_all | solution.py:45
  86.9 22.4 %all-to-all-start.1 = ((bf16[64,4,512]{2,1,0:T(4,128)(2,1)}), bf16[64,4,512]{2,1,0:T(4,128)(2,1)S(1)}, u32[]{:S(2)}, u32[]{:S(2)}) async-start(bf16[64,4,512]{2,1,0:T(4,128)(2,1)} %copy.121), calls=%async_computation.1 | async-start | bytes 524288 | tf_op jit(solution)/shard_map/all_to_all | solution.py:69
  109.3 6.7 %copy-start.7 = (bf16[64,4,512]{2,1,0:T(4,128)(2,1)}, bf16[64,4,512]{2,1,0:T(4,128)(2,1)S(1)}, u32[]{:S(2)}) copy-start(bf16[64,4,512]{2,1,0:T(4,128)(2,1)S(1)} %all-to-all-done.1) | copy-start | bytes 786436
  109.3 18.1 %all-to-all-start.3 = ((bf16[64,4,512]{2,1,0:T(4,128)(2,1)}), bf16[64,4,512]{2,1,0:T(4,128)(2,1)}, u32[]{:S(2)}, u32[]{:S(2)}) async-start(bf16[64,4,512]{2,1,0:T(4,128)(2,1)} %copy.126), calls=%async_computation.3 | async-start | bytes 524288 | tf_op jit(solution)/shard_map/all_to_all | solution.py:68
  121.5 7.4 %copy-start.2 = (f32[256,1,2,4,128]{0,4,3,2,1:T(8,128)S(1)}, f32[256,1,2,4,128]{0,4,3,2,1:T(8,128)}, u32[]{:S(2)}) copy-start(f32[256,1,2,4,128]{0,4,3,2,1:T(8,128)} %convolution_bitcast_fusion.2) | copy-start | bytes 3145732
  123.0 5.9 %copy-start.3 = (f32[256,1,2,4,128]{0,4,3,2,1:T(8,128)S(1)}, f32[256,1,2,4,128]{0,4,3,2,1:T(8,128)}, u32[]{:S(2)}) copy-start(f32[256,1,2,4,128]{0,4,3,2,1:T(8,128)} %convolution_bitcast_fusion.3) | copy-start | bytes 3145732
  129.3 1.7 copy-start.1
  131.1 73.0 %collective-permute-start = (f32[256,3,4,128]{0,3,2,1:T(8,128)S(1)}, f32[256,3,4,128]{0,3,2,1:T(8,128)}, u32[]{:S(2)}, u32[]{:S(2)}) collective-permute-start(f32[256,3,4,128]{0,3,2,1:T(8,128)S(1)} %dynamic-slice_bitcast_fusion), channel_id=1, source_target_pairs={{0,4},{1,5},{2,6},{3,7},{4,0},{5,1},{6,2},{7,3},{8,12},{9,13},{10,... | collective-permute-start | bytes 4718600 | tf_op jit(solution)/shard_map/ppermute | solution.py:10
  206.4 21.3 %collective-permute-start.1 = (f32[256,3,2,128]{0,3,2,1:T(8,128)S(1)}, f32[256,3,2,128]{0,3,2,1:T(8,128)}, u32[]{:S(2)}, u32[]{:S(2)}) collective-permute-start(f32[256,3,2,128]{0,3,2,1:T(8,128)S(1)} %dynamic-slice_bitcast_fusion.1), channel_id=1, source_target_pairs={{0,2},{1,3},{2,0},{3,1},{4,6},{5,7},{6,4},{7,5},{8,10},{9,11},{10,... | collective-permute-start | bytes 2359304 | tf_op jit(solution)/shard_map/ppermute | solution.py:10
  229.0 3.6 collective-permute-start.2
  232.6 3.6 collective-permute-start.3
  236.3 2.2 copy-start.4
  236.3 21.6 %collective-permute-start.4 = (f32[256,3,256]{0,2,1:T(8,128)S(1)}, f32[256,3,256]{0,2,1:T(8,128)}, u32[]{:S(2)}, u32[]{:S(2)}) collective-permute-start(f32[256,3,256]{0,2,1:T(8,128)S(1)} %maximum_select_fusion.2), channel_id=1, source_target_pairs={{0,2},{1,3},{2,0},{3,1},{4,6},{5,7},{6,4},{7,5},{8,10},{9,11},{10,... | collective-permute-start | bytes 2359304 | tf_op jit(solution)/shard_map/ppermute | solution.py:10
  260.0 72.5 %collective-permute-start.5 = (f32[256,3,512]{0,2,1:T(8,128)S(1)}, f32[256,3,512]{0,2,1:T(8,128)}, u32[]{:S(2)}, u32[]{:S(2)}) collective-permute-start(f32[256,3,512]{0,2,1:T(8,128)S(1)} %maximum_select_fusion.1), channel_id=1, source_target_pairs={{0,4},{1,5},{2,6},{3,7},{4,0},{5,1},{6,2},{7,3},{8,12},{9,13},{10,... | collective-permute-start | bytes 4718600 | tf_op jit(solution)/shard_map/ppermute | solution.py:10
  262.7 74.8 %all-to-all-start.6 = ((f32[64,1,4]{2,1,0:T(1,128)}), f32[64,1,4]{2,1,0:T(1,128)S(1)}, u32[]{:S(2)}, u32[]{:S(2)}) async-start(f32[64,1,4]{2,1,0:T(1,128)} %bitcast.45), calls=%async_computation.6 | async-start | bytes 65536 | tf_op jit(solution)/shard_map/all_to_all | solution.py:120
  270.4 64.4 %copy-start.5 = (bf16[1,512,1024]{2,1,0:T(8,128)(2,1)S(1)}, bf16[1,512,1024]{2,1,0:T(8,128)(2,1)}, u32[]{:S(2)}) copy-start(bf16[1,512,1024]{2,1,0:T(8,128)(2,1)} %param.11) | copy-start | bytes 3145732
  334.8 1.2 copy-start.6
  337.5 22.9 %all-to-all-start.4 = ((f32[64,4,512]{2,1,0:T(4,128)}), f32[64,4,512]{2,1,0:T(4,128)S(1)}, u32[]{:S(2)}, u32[]{:S(2)}) async-start(f32[64,4,512]{2,1,0:T(4,128)} %reshape.144), calls=%async_computation.4 | async-start | bytes 1048576 | tf_op jit(solution)/shard_map/all_to_all | solution.py:113
  360.4 19.0 %all-to-all-start.7 = ((f32[16,3,8]{2,1,0:T(4,128)}), f32[16,3,8]{2,1,0:T(4,128)S(1)}, u32[]{:S(2)}, u32[]{:S(2)}) async-start(f32[16,3,8]{2,1,0:T(4,128)} %copy.146), calls=%async_computation.7 | async-start | bytes 65536 | tf_op jit(solution)/shard_map/all_to_all | solution.py:137
  379.3 53.0 %all-to-all-start.5 = ((f32[16,3,4096]{2,1,0:T(4,128)}), f32[16,3,4096]{2,1,0:T(4,128)S(1)}, u32[]{:S(2)}, u32[]{:S(2)}) async-start(f32[16,3,4096]{2,1,0:T(4,128)} %copy.129), calls=%async_computation.5 | async-start | bytes 2097152 | tf_op jit(solution)/shard_map/all_to_all | solution.py:136
where the time goes:
time: 434 us; the launch traced here: 433 us
  waiting for transfers between devices  288 us (66%)
  starting transfers between devices  60.1 us (14%)
  blocking collectives  47.7 us (11%)
  local copies, waits for them, and re-layouts  17.6 us (4%)
  other arithmetic  12.7 us (3%)
  matrix products  6.3 us (1%)
    ppermute x6, waiting for transfers between devices, from_partner(): return lax.ppermute(value, axis, pairs)  174 us
    all_to_all x1, waiting for transfers between devices, body(): lax.all_to_all(token_grad, 'group', split_axis=0, concat_axis=0, tiled=True)  48.8 us
    all_to_all x1, blocking collectives, body(): lax.all_to_all(send_input, 'group', split_axis=0, concat_axis=0, tiled=True)  47.7 us
    all_to_all x1, waiting for transfers between devices, body(): lax.all_to_all(send_grad, 'group', split_axis=0, concat_axis=0, tiled=True)  25.4 us
    all_to_all x1, waiting for transfers between devices, body(): lax.all_to_all(returned.reshape(members, most, part_width), 'expert', spl...  15.1 us
    ppermute x6, starting transfers between devices, from_partner(): return lax.ppermute(value, axis, pairs)  12.6 us
    all_to_all x1, starting transfers between devices, body(): lax.all_to_all(pack_input, 'expert', split_axis=0, concat_axis=0, tiled=T...  10.8 us
    all_to_all x1, waiting for transfers between devices, body(): lax.all_to_all(pack_input, 'expert', split_axis=0, concat_axis=0, tiled=T...  9.69 us
  transfers between devices with their start and end apart: 13, of which 12 were waited for; matrix products, arithmetic and copies ran while one was open for 5% of the time, Pallas kernels for 0%

commit v1 on v0

v1 whole, which is shorter than its diff:
```python
import functools

import jax
import jax.numpy as jnp
from jax import lax
from jax.experimental import pallas as pl
from jax.experimental.pallas import tpu as pltpu
from jax.sharding import Mesh, PartitionSpec as P

BF = jnp.bfloat16
F32 = jnp.float32
MOST = 4
SPLIT = 8
ROWS = 2 * MOST
CORES = ("x", "yh", "yl", "c")
CHIPS = ("x", "yh", "yl")
ABT = (((1,), (1,)), ((), ()))


def dot(a, b):
    return jnp.dot(a, b, preferred_element_type=F32)


def dot_t(a, b):
    return lax.dot_general(a, b, ABT, preferred_element_type=F32)


def iota(shape, axis):
    return lax.broadcasted_iota(jnp.int32, shape, axis)


def call(kernel, out, limit_mib, *args, smem=0):
    spaces = [pltpu.SMEM] * smem + [pltpu.VMEM] * (len(args) - smem)
    many = isinstance(out, (list, tuple))
    outs = [pl.BlockSpec(memory_space=pltpu.VMEM) for _ in out] if many else None
    return pl.pallas_call(
        kernel,
        out_shape=out,
        in_specs=[pl.BlockSpec(memory_space=space) for space in spaces],
        out_specs=outs if many else pl.BlockSpec(memory_space=pltpu.VMEM),
        compiler_params=pltpu.CompilerParams(vmem_limit_bytes=limit_mib << 20),
    )(*args)


def payload_kernel(toks, width, x_ref, g_ref, o_ref):
    for tensor, ref in enumerate((x_ref, g_ref)):
        value = ref[...].astype(F32)
        for t in range(toks):
            rows = [value[t : t + 1, s * width : (s + 1) * width] for s in range(SPLIT)]
            at = (t * 2 + tensor) * width
            o_ref[:, at : at + width] = jnp.concatenate(rows, axis=0).astype(BF)


def rank_table(ids, first, experts):
    column = ids.shape[0]
    lane = iota((column, experts), 1)
    match = jnp.zeros((column, experts), F32)
    for e in range(experts):
        named = jnp.sum((ids == first + e).astype(F32), axis=1, keepdims=True)
        match = match + jnp.where(lane == e, named, 0.0)
    earlier = (iota((column, column), 1) < iota((column, column), 0)).astype(BF)
    rank = dot(earlier, match.astype(BF))
    return jnp.where(match > 0.0, rank, -1.0)


def row_fields(index, chips_y):
    slot = index % MOST
    part = (index // MOST) % (2 * chips_y)
    return index // (MOST * 2 * chips_y), part, slot


def pick_kernel(toks, experts, chips_y, first_ref, ids_ref, o_ref):
    _, rows, lanes = o_ref.shape
    column = ids_ref.shape[0]
    rank = rank_table(ids_ref[...], first_ref[0], experts).astype(BF)
    expert, _, _ = row_fields(iota((rows, experts), 0), chips_y)
    spread = dot_t((expert == iota((rows, experts), 1)).astype(BF), rank).astype(BF)
    _, part, slot = row_fields(iota((rows, lanes), 0), chips_y)
    same_part = part == iota((rows, lanes), 1) % SPLIT
    tok = iota((column, lanes), 0)
    group = iota((column, lanes), 1) // SPLIT
    for t in range(toks):
        table = dot(spread, (tok == group * toks + t).astype(BF))
        o_ref[t] = (same_part & (table == slot.astype(F32))).astype(BF)


def merge_kernel(toks, experts, chips_y, first_ref, ids_ref, w_ref, hi_ref, lo_ref, pick_ref):
    _, rows, lanes = hi_ref.shape
    column = ids_ref.shape[0]
    ids = ids_ref[...]
    first = first_ref[0]
    rank = rank_table(ids, first, experts).astype(BF)
    weights = w_ref[...]
    lane = iota((column, experts), 1)
    scale = jnp.zeros((column, experts), F32)
    for e in range(experts):
        named = jnp.sum(jnp.where(ids == first + e, weights, 0.0), axis=1, keepdims=True)
        scale = scale + jnp.where(lane == e, named, 0.0)
    scale_hi = scale.astype(BF)
    scale_lo = (scale - scale_hi.astype(F32)).astype(BF)
    expert, _, _ = row_fields(iota((experts, lanes), 1), chips_y)
    spread = (expert == iota((experts, lanes), 0)).astype(BF)
    far = dot(rank, spread).astype(BF)
    far_hi = dot(scale_hi, spread).astype(BF)
    far_lo = dot(scale_lo, spread).astype(BF)
    expert, part, slot = row_fields(iota((rows, lanes), 1), chips_y)
    same_part = part == iota((rows, lanes), 0) % SPLIT
    slot = slot.astype(F32)
    names = first + expert
    tok = iota((rows, column), 1)
    group = iota((rows, column), 0) // SPLIT
    top = ids.shape[1]
    route = iota((rows, top), 1) == iota((rows, top), 0) % SPLIT
    low = ids.astype(F32).astype(BF)
    for t in range(toks):
        at = (tok == group * toks + t).astype(BF)
        held = dot(at, far) == slot
        both = held & same_part
        hi_ref[t] = jnp.where(both, dot(at, far_hi), 0.0).astype(BF)
        lo_ref[t] = jnp.where(both, dot(at, far_lo), 0.0).astype(BF)
        name = jnp.sum(jnp.where(route, dot(at, low), 0.0), axis=1, keepdims=True)
        mine = name == names.astype(F32)
        pick_ref[t] = (held & mine & (part == 0)).astype(BF)


def pack_kernel(pick_ref, tokens_ref, o_ref):
    toks = pick_ref.shape[0]
    width = tokens_ref.shape[1] // toks
    total = dot(pick_ref[0], tokens_ref[:, :width])
    for t in range(1, toks):
        total = total + dot(pick_ref[t], tokens_ref[:, t * width : (t + 1) * width])
    o_ref[...] = total.astype(BF)


def scaled(value):
    largest = jnp.max(jnp.abs(value), axis=1, keepdims=True)
    power = jnp.where(largest > 0.0, jnp.floor(jnp.log2(jnp.maximum(largest, 1e-30))), 0.0)
    return value * jnp.exp2(-power), power


def partial_kernel(core_ref, rows_ref, go_ref, gt_ref, uo_ref, ut_ref, do_ref, dt_ref, o_ref):
    core = core_ref[0]
    both, width2 = rows_ref.shape
    width, hidden = go_ref.shape
    rows = both // 2
    q = iota((both, both), 0)
    half = jnp.where(q < rows, core, 1 - core)
    q = q % rows
    source = (q // MOST) * ROWS + half * MOST + q % MOST
    order = (source == iota((both, both), 1)).astype(BF)
    held = dot(order, rows_ref[...]).astype(BF)
    x_own, x_other = held[:rows, :width], held[rows:, :width]
    g_own, g_other = held[:rows, width:], held[rows:, width:]
    gate, gate_power = scaled(dot(x_own, go_ref[...]) + dot(x_other, gt_ref[...]))
    o_ref[:, :hidden] = gate
    up, up_power = scaled(dot(x_own, uo_ref[...]) + dot(x_other, ut_ref[...]))
    o_ref[:, hidden : 2 * hidden] = up
    down, down_power = scaled(dot_t(g_own, do_ref[...]) + dot_t(g_other, dt_ref[...]))
    o_ref[:, 2 * hidden : 3 * hidden] = down
    lane = iota((rows, 128), 1)
    powers = jnp.where(lane == 0, gate_power, jnp.where(lane == 1, up_power, down_power))
    o_ref[:, 3 * hidden :] = powers


def hidden_kernel(hidden, p_ref, o_ref):
    def total(which):
        value = None
        for j in range(p_ref.shape[0]):
            at = 3 * hidden + which
            factor = jnp.exp2(p_ref[j, :, 3 * hidden :][:, which : which + 1])
            term = p_ref[j, :, which * hidden : (which + 1) * hidden] * factor
            value = term if value is None else value + term
        return value

    a, b, r = total(0), total(1), total(2)
    sig = jax.nn.sigmoid(a)
    silu = a * sig
    o_ref[:, :hidden] = (r * b * (sig * (1.0 + a * (1.0 - sig)))).astype(BF)
    o_ref[:, hidden : 2 * hidden] = (r * silu).astype(BF)
    route = jnp.sum(silu * b * r, axis=1, keepdims=True)
    hi = route.astype(BF).astype(F32)
    mid = (route - hi).astype(BF).astype(F32)
    lo = route - hi - mid
    lane = iota((route.shape[0], 128), 1)
    pieces = jnp.where(lane == 0, hi, jnp.where(lane == 1, mid, jnp.where(lane == 2, lo, 0.0)))
    o_ref[:, 2 * hidden :] = pieces.astype(BF)


def return_kernel(core_ref, d_ref, go_ref, gt_ref, uo_ref, ut_ref, o_ref):
    core = core_ref[0]
    width, hidden = go_ref.shape
    rows = d_ref.shape[0]
    d_gate = d_ref[:, :hidden]
    d_up = d_ref[:, hidden : 2 * hidden]
    own = (dot_t(d_gate, go_ref[...]) + dot_t(d_up, uo_ref[...])).astype(BF)
    other = (dot_t(d_gate, gt_ref[...]) + dot_t(d_up, ut_ref[...])).astype(BF)
    q = iota((2 * rows, rows), 0)
    here = (q // ROWS) * MOST + q % MOST == iota((2 * rows, rows), 1)
    mine = (q // MOST) % 2 == core
    to_own = (here & mine).astype(BF)
    to_other = (here & ~mine).astype(BF)
    o_ref[:, :width] = (dot(to_own, own) + dot(to_other, other)).astype(BF)
    o_ref[:, width:] = dot(here.astype(BF), d_ref[:, 2 * hidden :]).astype(BF)


def combine_kernel(hi_ref, lo_ref, pick_ref, b_ref, o_ref):
    toks, rows, _ = hi_ref.shape
    width = b_ref.shape[1] - 128
    value = b_ref[:, :width]
    extra = b_ref[:, width:]
    lane = iota((rows, 128), 1)
    routes = jnp.zeros((rows, 128), F32)
    for t in range(toks):
        total = dot(hi_ref[t], value) + dot(lo_ref[t], value)
        o_ref[:, t * width : (t + 1) * width] = total.astype(BF)
        route = jnp.sum(dot(pick_ref[t], extra), axis=1, keepdims=True)
        hi = route.astype(BF).astype(F32)
        routes = jnp.where(lane == 2 * t, hi, jnp.where(lane == 2 * t + 1, route - hi, routes))
    o_ref[:, toks * width :] = routes.astype(BF)


def home_kernel(toks, width, h_ref, x_ref, r_ref):
    total = h_ref[0].astype(F32)
    for g in range(1, h_ref.shape[0]):
        total = total + h_ref[g].astype(F32)
    top = r_ref.shape[1]
    extra = total[:, toks * width :]
    lane = iota(extra.shape, 1)
    diagonal = iota((SPLIT, top), 0) == iota((SPLIT, top), 1)
    for t in range(toks):
        for s in range(SPLIT):
            x_ref[t : t + 1, s * width : (s + 1) * width] = total[
                s : s + 1, t * width : (t + 1) * width
            ]
        route = jnp.sum(jnp.where(lane // 2 == t, extra, 0.0), axis=1, keepdims=True)
        r_ref[t : t + 1, :] = jnp.sum(jnp.where(diagonal, route, 0.0), axis=0, keepdims=True)


def body(grad_out, inputs, expert_ids, route_weights, w_gate, w_up, w_down):
    groups = lax.axis_size("z")
    chips_y = lax.axis_size("yl")
    experts = lax.axis_size("x") * lax.axis_size("yh")
    chips = experts * chips_y
    toks = grad_out.shape[1]
    width, hidden = w_gate.shape[1:]
    top = expert_ids.shape[2]
    core = lax.axis_index("c").astype(jnp.int32).reshape(1)
    first = (lax.axis_index("z") * experts).astype(jnp.int32).reshape(1)
    held = groups * SPLIT
    sent = chips * ROWS
    rows = chips * MOST

    swap = [(0, 1), (1, 0)]
    wg, wu, wd = w_gate[0], w_up[0], w_down[0]
    wg_other = lax.ppermute(wg, "c", swap)
    wu_other = lax.ppermute(wu, "c", swap)
    wd_other = lax.ppermute(wd, "c", swap)

    payload = call(
        functools.partial(payload_kernel, toks, width),
        jax.ShapeDtypeStruct((SPLIT, 2 * toks * width), BF),
        16,
        inputs[0],
        grad_out[0],
    )
    tokens = lax.all_gather(payload, "z", axis=0, tiled=False).reshape(held, -1)

    pick = call(
        functools.partial(pick_kernel, toks, experts, chips_y),
        jax.ShapeDtypeStruct((toks, sent, held), BF),
        16,
        first,
        expert_ids[0],
        smem=1,
    )
    merged = jax.ShapeDtypeStruct((toks, held, sent), BF)
    merge_hi, merge_lo, merge_pick = call(
        functools.partial(merge_kernel, toks, experts, chips_y),
        [merged, merged, merged],
        16,
        first,
        expert_ids[0],
        route_weights[0],
        smem=1,
    )

    packed = call(pack_kernel, jax.ShapeDtypeStruct((sent, 2 * width), BF), 16, pick, tokens)
    got = lax.all_to_all(
        packed.reshape(chips, ROWS, 2 * width), CHIPS, split_axis=0, concat_axis=0, tiled=True
    ).reshape(sent, 2 * width)

    partials = call(
        partial_kernel,
        jax.ShapeDtypeStruct((rows, 3 * hidden + 128), F32),
        32,
        core,
        got,
        wg,
        wg_other,
        wu,
        wu_other,
        wd,
        wd_other,
        smem=1,
    )
    shares = partials.astype(jnp.float16).reshape(chips_y, rows // chips_y, -1)
    shares = lax.all_to_all(shares, "yl", split_axis=0, concat_axis=0, tiled=True)
    grads = call(
        functools.partial(hidden_kernel, hidden),
        jax.ShapeDtypeStruct((rows // chips_y, 2 * hidden + 128), BF),
        16,
        shares.astype(F32),
    )
    all_grads = lax.all_gather(grads, "yl", axis=0, tiled=True)

    back = call(
        return_kernel,
        jax.ShapeDtypeStruct((sent, width + 128), BF),
        32,
        core,
        all_grads,
        wg,
        wg_other,
        wu,
        wu_other,
        smem=1,
    )
    back = lax.all_to_all(
        back.reshape(chips, ROWS, -1), CHIPS, split_axis=0, concat_axis=0, tiled=True
    ).reshape(sent, -1)

    home = call(
        combine_kernel,
        jax.ShapeDtypeStruct((held, toks * width + 128), BF),
        16,
        merge_hi,
        merge_lo,
        merge_pick,
        back,
    )
    home = lax.all_to_all(
        home.reshape(groups, SPLIT, -1), "z", split_axis=0, concat_axis=0, tiled=True
    )
    grad_in, grad_route = call(
        functools.partial(home_kernel, toks, width),
        [
            jax.ShapeDtypeStruct((toks, SPLIT * width), F32),
            jax.ShapeDtypeStruct((toks, top), F32),
        ],
        16,
        home,
    )
    return grad_in[None], grad_route[None]


def solution(mesh):
    groups, members = mesh.devices.shape
    chips_y = SPLIT // 2
    x = 4 if members == 64 else 2
    fine = Mesh(
        mesh.devices.reshape(groups, x, members // (x * SPLIT), chips_y, 2), ("z",) + CORES
    )
    tokens = P(CORES, "z", None)
    tables = P(CORES, None, None)
    weights = P(("z",) + CORES, None, None)
    return jax.shard_map(
        body,
        mesh=fine,
        in_specs=(tokens, tokens, tables, tables, weights, weights, weights),
        out_specs=(tokens, tokens),
        check_vma=False,
    )
```

time: 434 us -> 171 us (0.39)
  the two profiles are of different devices: /device:TPU:6 before, /device:TPU:72 now
where the time goes in v1:
time: 171 us; the launch traced here: 170 us
  blocking collectives  105 us (61%)
  waiting for transfers between devices  24.3 us (14%)
  starting transfers between devices  23.3 us (14%)
  Pallas kernels  10 us (6%)
  local copies, waits for them, and re-layouts  6.75 us (4%)
    all_gather x1, blocking collectives, body(): tokens = lax.all_gather(payload, 'z', axis=0, tiled=False).reshape(held, -1)  46.2 us
    all_to_all x1, blocking collectives, body(): lax.all_to_all(home.reshape(groups, SPLIT, -1), 'z', split_axis=0, concat...  23.6 us
    all_to_all x1, blocking collectives, body(): lax.all_to_all(shares, 'yl', split_axis=0, concat_axis=0, tiled=True)  19.6 us
    all_gather x1, blocking collectives, body(): all_grads = lax.all_gather(grads, 'yl', axis=0, tiled=True)  15.6 us
    all_to_all x1, waiting for transfers between devices, body(): lax.all_to_all(packed.reshape(chips, ROWS, 2 * width), CHIPS, split_axis=...  13.5 us
    all_to_all x1, waiting for transfers between devices, body(): lax.all_to_all(back.reshape(chips, ROWS, -1), CHIPS, split_axis=0, concat...  10.8 us
    all_to_all x1, starting transfers between devices, body(): lax.all_to_all(packed.reshape(chips, ROWS, 2 * width), CHIPS, split_axis=...  10.2 us
    pallas_call x9, Pallas kernels, call(): pl.pallas_call(kernel, out_shape=out, in_specs=[pl.BlockSpec(memory_space...  10 us
  transfers between devices with their start and end apart: 5, of which 2 were waited for; matrix products, arithmetic and copies ran while one was open for 0% of the time, Pallas kernels for 1%

profile of v1, /device:TPU:72, one launch (start us, length us, event | category | flops | bytes accessed | tf_op | source)
XLA Modules:
  0.0 170.4 jit_solution(5024571336720655506)
XLA Ops:
  0.6 1.9 %collective-permute-start = (bf16[512,1024]{1,0:T(8,128)(2,1)}, bf16[512,1024]{1,0:T(8,128)(2,1)S(1)}, u32[]{:S(2)}, u32[]{:S(2)}) collective-permute-start(bf16[512,1024]{1,0:T(8,128)(2,1)} %bitcast.17), channel_id=1, source_target_pairs={{0,1},{1,0},{2,3},{3,2},{4,5},{5,4},{6,7},{7,6},{8,9},{9,8},{10,11... | collective-permute-start | bytes 3145736 | tf_op jit(solution)/shard_map/ppermute | solution.py:255
  2.6 2.4 %collective-permute-start.1 = (bf16[512,1024]{1,0:T(8,128)(2,1)}, bf16[512,1024]{1,0:T(8,128)(2,1)}, u32[]{:S(2)}, u32[]{:S(2)}) collective-permute-start(bf16[512,1024]{1,0:T(8,128)(2,1)} %bitcast.20), channel_id=1, source_target_pairs={{0,1},{1,0},{2,3},{3,2},{4,5},{5,4},{6,7},{7,6},{8,9},{9,8},{10,11... | collective-permute-start | bytes 3145736 | tf_op jit(solution)/shard_map/ppermute | solution.py:256
  5.0 1.9 %collective-permute-start.2 = (bf16[1024,512]{1,0:T(8,128)(2,1)}, bf16[1024,512]{1,0:T(8,128)(2,1)}, u32[]{:S(2)}, u32[]{:S(2)}) collective-permute-start(bf16[1024,512]{1,0:T(8,128)(2,1)} %bitcast.26), channel_id=1, source_target_pairs={{0,1},{1,0},{2,3},{3,2},{4,5},{5,4},{6,7},{7,6},{8,9},{9,8},{10,11... | collective-permute-start | bytes 3145736 | tf_op jit(solution)/shard_map/ppermute | solution.py:257
  6.9 0.0 copy-start.5
  6.9 0.7 copy-done.5
  7.7 0.0 copy-start.6
  7.7 0.8 copy-done.6
  8.4 0.1 shard_map.88
  8.5 0.0 copy-start
  8.5 0.0 copy-start.1
  8.5 46.2 %all-gather.tokens_ref = bf16[128,3072]{1,0:T(8,128)(2,1)} all-gather(bf16[8,3072]{1,0:T(8,128)(2,1)S(1)} %shard_map.88), channel_id=2, replica_groups=mesh['z'=16,'x'=4,'yh'=2,'yl'=4,'c'=2] {'z'}, dimensions={0}, use_global_device_ids=true | all-gather | bytes 835584 | tf_op jit(solution)/shard_map/all_gather | solution.py:266
  54.7 0.8 copy.9
  55.4 0.6 shard_map.87.pick_ref
  56.0 0.0 copy-start.2
  56.0 1.1 copy-done.2
  57.1 0.5 shard_map.89
  57.7 0.0 copy-start.3
  57.7 0.8 copy-done.3
  58.5 10.2 %all-to-all-start = ((bf16[32,8,1024]{2,1,0:T(8,128)(2,1)}), bf16[32,8,1024]{2,1,0:T(8,128)(2,1)}, u32[]{:S(2)}, u32[]{:S(2)}) async-start(bf16[32,8,1024]{2,1,0:T(8,128)(2,1)} %bitcast.23), calls=%async_computation | async-start | bytes 1048576 | tf_op jit(solution)/shard_map/all_to_all | solution.py:288
  68.7 13.5 %all-to-all-done = bf16[32,8,1024]{2,1,0:T(8,128)(2,1)} async-done(((bf16[32,8,1024]{2,1,0:T(8,128)(2,1)}), bf16[32,8,1024]{2,1,0:T(8,128)(2,1)}, u32[]{:S(2)}, u32[]{:S(2)}) %all-to-all-start) | async-done | bytes 524320 | tf_op jit(solution)/shard_map/all_to_all | solution.py:288
  82.2 0.0 collective-permute-done.gt_ref
  82.2 0.0 collective-permute-done.1.ut_ref
  82.2 0.0 collective-permute-done.2.dt_ref
  82.3 0.0 copy-done
  82.3 0.0 copy-done.1
  82.3 0.0 copy-start.4
  82.3 1.2 copy-done.4
  83.5 3.4 %shard_map.90 = f32[128,3200]{1,0:T(8,128)S(1)} custom-call(s32[1]{0:T(128)} %bitcast.3.core_ref, bf16[256,1024]{1,0:T(8,128)(2,1)} %bitcast.7.rows_ref, bf16[512,1024]{1,0:T(8,128)(2,1)S(1)} %bitcast.18, bf16[512,1024]{1,0:T(8,128)(2,1)S(1)} %collective-permute-done.gt_ref, bf16[512,1024]{1,0:T(8,128)(2,1)S(1)} %bitcast.21, ...), custom_call_target="tpu_custom_call" | custom-call | tf_op jit(solution)/shard_map/pallas_call | solution.py:36
  86.9 0.1 convert_element_type.6
  87.0 19.6 %all_to_all.20 = f16[4,32,3200]{2,1,0:T(8,128)(2,1)S(1)} all-to-all(f16[4,32,3200]{2,1,0:T(8,128)(2,1)S(1)} %bitcast.35), channel_id=1, replica_groups=mesh['z'=16,'x'=4,'yh'=2,'yl'=4,'c'=2] {'yl'}, dimensions={0} | all-to-all | bytes 1638400 | tf_op jit(solution)/shard_map/all_to_all | solution.py:307
  106.6 0.1 convert_element_type.7.p_ref
  106.7 0.3 shard_map.91
  107.0 15.6 %all_gather.11.d_ref = bf16[128,2176]{1,0:T(8,128)(2,1)S(1)} all-gather(bf16[32,2176]{1,0:T(8,128)(2,1)S(1)} %shard_map.91), channel_id=1, replica_groups=mesh['z'=16,'x'=4,'yh'=2,'yl'=4,'c'=2] {'yl'}, dimensions={0}, use_global_device_ids=true | all-gather | bytes 696320 | tf_op jit(solution)/shard_map/all_gather | solution.py:314
  122.7 0.0 copy-start.7
  122.7 3.8 %shard_map.92 = bf16[256,640]{1,0:T(8,128)(2,1)} custom-call(s32[1]{0:T(128)} %bitcast.3.core_ref, bf16[128,2176]{1,0:T(8,128)(2,1)S(1)} %all_gather.11.d_ref, bf16[512,1024]{1,0:T(8,128)(2,1)S(1)} %bitcast.19, bf16[512,1024]{1,0:T(8,128)(2,1)S(1)} %collective-permute-done.gt_ref, bf16[512,1024]{1,0:T(8,128)(2,1)S(1)} %bitcast.22, ...), custom_call_target="tpu_custom_call" | custom-call | tf_op jit(solution)/shard_map/pallas_call | solution.py:36
  126.4 6.8 %all-to-all-start.2 = ((bf16[32,8,640]{2,1,0:T(8,128)(2,1)}), bf16[32,8,640]{2,1,0:T(8,128)(2,1)S(1)}, u32[]{:S(2)}, u32[]{:S(2)}) async-start(bf16[32,8,640]{2,1,0:T(8,128)(2,1)} %bitcast.12), calls=%async_computation.2 | async-start | bytes 655360 | tf_op jit(solution)/shard_map/all_to_all | solution.py:328
  133.3 0.0 copy-done.7
  133.3 0.1 copy.10
  133.4 0.8 shard_map.86
  134.2 10.8 %all-to-all-done.2 = bf16[32,8,640]{2,1,0:T(8,128)(2,1)S(1)} async-done(((bf16[32,8,640]{2,1,0:T(8,128)(2,1)}), bf16[32,8,640]{2,1,0:T(8,128)(2,1)S(1)}, u32[]{:S(2)}, u32[]{:S(2)}) %all-to-all-start.2) | async-done | bytes 327712 | tf_op jit(solution)/shard_map/all_to_all | solution.py:328
  145.0 0.5 shard_map.93
  145.5 23.6 %all_to_all.21.h_ref = bf16[16,8,1664]{2,1,0:T(8,128)(2,1)S(1)} all-to-all(bf16[16,8,1664]{2,1,0:T(8,128)(2,1)S(1)} %bitcast.24), channel_id=1, replica_groups=mesh['z'=16,'x'=4,'yh'=2,'yl'=4,'c'=2] {'z'}, dimensions={0} | all-to-all | bytes 851968 | tf_op jit(solution)/shard_map/all_to_all | solution.py:341
  169.1 0.1 shard_map.94
  169.2 0.7 copy.11
  169.8 0.6 copy.12
Async XLA Ops:
  0.6 81.6 %collective-permute-start = (bf16[512,1024]{1,0:T(8,128)(2,1)}, bf16[512,1024]{1,0:T(8,128)(2,1)S(1)}, u32[]{:S(2)}, u32[]{:S(2)}) collective-permute-start(bf16[512,1024]{1,0:T(8,128)(2,1)} %bitcast.17), channel_id=1, source_target_pairs={{0,1},{1,0},{2,3},{3,2},{4,5},{5,4},{6,7},{7,6},{8,9},{9,8},{10,11... | collective-permute-start | bytes 3145736 | tf_op jit(solution)/shard_map/ppermute | solution.py:255
  2.6 79.7 %collective-permute-start.1 = (bf16[512,1024]{1,0:T(8,128)(2,1)}, bf16[512,1024]{1,0:T(8,128)(2,1)}, u32[]{:S(2)}, u32[]{:S(2)}) collective-permute-start(bf16[512,1024]{1,0:T(8,128)(2,1)} %bitcast.20), channel_id=1, source_target_pairs={{0,1},{1,0},{2,3},{3,2},{4,5},{5,4},{6,7},{7,6},{8,9},{9,8},{10,11... | collective-permute-start | bytes 3145736 | tf_op jit(solution)/shard_map/ppermute | solution.py:256
  5.0 77.3 %collective-permute-start.2 = (bf16[1024,512]{1,0:T(8,128)(2,1)}, bf16[1024,512]{1,0:T(8,128)(2,1)}, u32[]{:S(2)}, u32[]{:S(2)}) collective-permute-start(bf16[1024,512]{1,0:T(8,128)(2,1)} %bitcast.26), channel_id=1, source_target_pairs={{0,1},{1,0},{2,3},{3,2},{4,5},{5,4},{6,7},{7,6},{8,9},{9,8},{10,11... | collective-permute-start | bytes 3145736 | tf_op jit(solution)/shard_map/ppermute | solution.py:257
  6.9 0.8 copy-start.5
  7.7 0.8 copy-start.6
  8.5 73.8 %copy-start = (bf16[1,512,1024]{2,1,0:T(8,128)(2,1)S(1)}, bf16[1,512,1024]{2,1,0:T(8,128)(2,1)}, u32[]{:S(2)}) copy-start(bf16[1,512,1024]{2,1,0:T(8,128)(2,1)} %param.11) | copy-start | bytes 3145732
  8.5 73.8 %copy-start.1 = (bf16[1,512,1024]{2,1,0:T(8,128)(2,1)S(1)}, bf16[1,512,1024]{2,1,0:T(8,128)(2,1)}, u32[]{:S(2)}) copy-start(bf16[1,512,1024]{2,1,0:T(8,128)(2,1)} %param.12) | copy-start | bytes 3145732
  56.0 1.1 copy-start.2
  57.7 0.8 copy-start.3
  58.5 23.7 %all-to-all-start = ((bf16[32,8,1024]{2,1,0:T(8,128)(2,1)}), bf16[32,8,1024]{2,1,0:T(8,128)(2,1)}, u32[]{:S(2)}, u32[]{:S(2)}) async-start(bf16[32,8,1024]{2,1,0:T(8,128)(2,1)} %bitcast.23), calls=%async_computation | async-start | bytes 1048576 | tf_op jit(solution)/shard_map/all_to_all | solution.py:288
  82.3 1.2 copy-start.4
  122.7 10.6 %copy-start.7 = (f32[1,48,8]{1,2,0:T(8,128)S(1)}, f32[1,48,8]{1,2,0:T(8,128)}, u32[]{:S(2)}) copy-start(f32[1,48,8]{1,2,0:T(8,128)} %param.10) | copy-start | bytes 4612
  126.4 18.5 %all-to-all-start.2 = ((bf16[32,8,640]{2,1,0:T(8,128)(2,1)}), bf16[32,8,640]{2,1,0:T(8,128)(2,1)S(1)}, u32[]{:S(2)}, u32[]{:S(2)}) async-start(bf16[32,8,640]{2,1,0:T(8,128)(2,1)} %bitcast.12), calls=%async_computation.2 | async-start | bytes 655360 | tf_op jit(solution)/shard_map/all_to_all | solution.py:328

commit v2 on v1

v2 whole, which is shorter than its diff:
```python
import functools

import jax
import jax.numpy as jnp
from jax import lax
from jax.experimental import pallas as pl
from jax.experimental.pallas import tpu as pltpu
from jax.sharding import Mesh, PartitionSpec as P

BF = jnp.bfloat16
F32 = jnp.float32
MOST = 4
SPLIT = 8
ROWS = 2 * MOST
CORES = ("x", "yh", "yl", "c")
CHIPS = ("x", "yh", "yl")
ABT = (((1,), (1,)), ((), ()))


def dot(a, b):
    return jnp.dot(a, b, preferred_element_type=F32)


def dot_t(a, b):
    return lax.dot_general(a, b, ABT, preferred_element_type=F32)


def iota(shape, axis):
    return lax.broadcasted_iota(jnp.int32, shape, axis)


def call(kernel, out, limit_mib, *args, smem=0, hbm=0, scratch=()):
    inside = len(args) - smem - hbm
    spaces = [pltpu.SMEM] * smem + [pltpu.VMEM] * inside + [pltpu.HBM] * hbm
    many = isinstance(out, (list, tuple))
    outs = [pl.BlockSpec(memory_space=pltpu.VMEM) for _ in out] if many else None
    return pl.pallas_call(
        kernel,
        out_shape=out,
        in_specs=[pl.BlockSpec(memory_space=space) for space in spaces],
        out_specs=outs if many else pl.BlockSpec(memory_space=pltpu.VMEM),
        scratch_shapes=scratch,
        compiler_params=pltpu.CompilerParams(vmem_limit_bytes=limit_mib << 20),
    )(*args)


def weight_places(width, hidden):
    return (
        (pl.ds(0, width), pl.ds(width, hidden)),
        (pl.ds(width, width), pl.ds(width, hidden)),
        (pl.ds(0, hidden), pl.ds(0, width)),
    )


def bring(source, room, sems, places):
    copies = [
        pltpu.make_async_copy(source.at[place], room.at[place], sems.at[i])
        for i, place in enumerate(places)
    ]
    for copy in copies:
        copy.start()
    return copies


def start_kernel(toks, x_hbm, g_hbm, wg_hbm, wu_hbm, wd_hbm, o_ref, all_hbm, held, room, sems):
    width, hidden = wg_hbm.shape[1:]
    copies = [
        pltpu.make_async_copy(ref, held.at[i], sems.at[i]) for i, ref in enumerate((x_hbm, g_hbm))
    ]
    moves = [
        (
            pltpu.make_async_copy(ref.at[0], room.at[place], sems.at[2 + i]),
            pltpu.make_async_copy(room.at[place], all_hbm.at[place], sems.at[5 + i]),
        )
        for i, (ref, place) in enumerate(
            zip((wg_hbm, wu_hbm, wd_hbm), weight_places(width, hidden))
        )
    ]
    for copy in copies + [come for come, _ in moves]:
        copy.start()
    for tensor, copy in enumerate(copies):
        copy.wait()
        value = held[tensor, 0].astype(F32)
        for t in range(toks):
            rows = [value[t : t + 1, s * width : (s + 1) * width] for s in range(SPLIT)]
            at = (t * 2 + tensor) * width
            o_ref[:, at : at + width] = jnp.concatenate(rows, axis=0).astype(BF)
    for come, go in moves:
        come.wait()
        go.start()
    for _, go in moves:
        go.wait()


def spread_rows(rows):
    at = iota((len(rows), rows[0].shape[1]), 0)
    value = jnp.zeros(at.shape, F32)
    for e, row in enumerate(rows):
        value = value + jnp.where(at == e, row, 0.0)
    return value


def rank_table(ids, first, experts):
    column = ids.shape[1]
    match = spread_rows(
        [
            jnp.sum((ids == first + e).astype(F32), axis=0, keepdims=True)
            for e in range(experts)
        ]
    )
    earlier = (iota((column, column), 0) < iota((column, column), 1)).astype(BF)
    rank = dot(match.astype(BF), earlier)
    return jnp.where(match > 0.0, rank, -1.0)


def row_fields(index, chips_y):
    slot = index % MOST
    part = (index // MOST) % (2 * chips_y)
    return index // (MOST * 2 * chips_y), part, slot


def pick_kernel(toks, experts, chips_y, first_ref, ids_ref, o_ref):
    _, rows, lanes = o_ref.shape
    column = ids_ref.shape[1]
    rank = rank_table(ids_ref[...], first_ref[0], experts).astype(BF)
    expert, _, _ = row_fields(iota((rows, experts), 0), chips_y)
    spread = dot((expert == iota((rows, experts), 1)).astype(BF), rank).astype(BF)
    _, part, slot = row_fields(iota((rows, lanes), 0), chips_y)
    same_part = part == iota((rows, lanes), 1) % SPLIT
    tok = iota((column, lanes), 0)
    group = iota((column, lanes), 1) // SPLIT
    for t in range(toks):
        table = dot(spread, (tok == group * toks + t).astype(BF))
        o_ref[t] = (same_part & (table == slot.astype(F32))).astype(BF)


def merge_kernel(toks, experts, chips_y, first_ref, ids_ref, w_ref, hi_ref, lo_ref, pick_ref):
    _, rows, lanes = hi_ref.shape
    column = ids_ref.shape[1]
    ids = ids_ref[...]
    first = first_ref[0]
    rank = rank_table(ids, first, experts).astype(BF)
    weights = w_ref[...]
    scale = spread_rows(
        [
            jnp.sum(jnp.where(ids == first + e, weights, 0.0), axis=0, keepdims=True)
            for e in range(experts)
        ]
    )
    scale_hi = scale.astype(BF)
    scale_lo = (scale - scale_hi.astype(F32)).astype(BF)
    expert, _, _ = row_fields(iota((experts, lanes), 1), chips_y)
    spread = (expert == iota((experts, lanes), 0)).astype(BF)
    expert, part, slot = row_fields(iota((rows, lanes), 1), chips_y)
    same_part = part == iota((rows, lanes), 0) % SPLIT
    slot = slot.astype(F32)
    names = (first + expert).astype(F32)
    tok = iota((rows, column), 1)
    group = iota((rows, column), 0) // SPLIT
    top = ids.shape[0]
    route = iota((rows, top), 1) == iota((rows, top), 0) % SPLIT
    low = ids.astype(F32).astype(BF)
    for t in range(toks):
        at = (tok == group * toks + t).astype(BF)
        held = dot(dot_t(at, rank).astype(BF), spread) == slot
        both = held & same_part
        hi_ref[t] = jnp.where(both, dot(dot_t(at, scale_hi).astype(BF), spread), 0.0).astype(BF)
        lo_ref[t] = jnp.where(both, dot(dot_t(at, scale_lo).astype(BF), spread), 0.0).astype(BF)
        name = jnp.sum(jnp.where(route, dot_t(at, low), 0.0), axis=1, keepdims=True)
        pick_ref[t] = (held & (name == names) & (part == 0)).astype(BF)


def pack_kernel(pick_ref, tokens_ref, o_ref):
    toks = pick_ref.shape[0]
    groups, split, lanes = tokens_ref.shape
    width = lanes // toks
    total = None
    for t in range(toks):
        tokens = tokens_ref[:, :, t * width : (t + 1) * width].reshape(groups * split, width)
        term = dot(pick_ref[t], tokens)
        total = term if total is None else total + term
    o_ref[...] = total.astype(BF)


def scaled(value):
    largest = jnp.max(jnp.abs(value), axis=1, keepdims=True)
    power = jnp.where(largest > 0.0, jnp.floor(jnp.log2(jnp.maximum(largest, 1e-30))), 0.0)
    return value * jnp.exp2(-power), power


def partial_kernel(core_ref, rows_ref, own_ref, other_hbm, o_ref, other_ref, sems):
    core = core_ref[0]
    both = rows_ref.shape[0]
    hidden = own_ref.shape[0]
    width = own_ref.shape[1] - hidden
    places = weight_places(width, hidden)
    copies = bring(other_hbm, other_ref, sems, places)
    rows = both // 2
    q = iota((both, both), 0)
    half = jnp.where(q < rows, core, 1 - core)
    q = q % rows
    source = (q // MOST) * ROWS + half * MOST + q % MOST
    order = (source == iota((both, both), 1)).astype(BF)
    held = dot(order, rows_ref[...]).astype(BF)
    x_own, x_other = held[:rows, :width], held[rows:, :width]
    g_own, g_other = held[:rows, width:], held[rows:, width:]
    gate = dot(x_own, own_ref[:width, width:])
    up = dot(x_own, own_ref[width:, width:])
    down = dot_t(g_own, own_ref[:, :width])
    copies[0].wait()
    gate, gate_power = scaled(gate + dot(x_other, other_ref[:width, width:]))
    o_ref[:, :hidden] = gate
    copies[1].wait()
    up, up_power = scaled(up + dot(x_other, other_ref[width:, width:]))
    o_ref[:, hidden : 2 * hidden] = up
    copies[2].wait()
    down, down_power = scaled(down + dot_t(g_other, other_ref[:, :width]))
    o_ref[:, 2 * hidden : 3 * hidden] = down
    lane = iota((rows, 128), 1)
    powers = jnp.where(lane == 0, gate_power, jnp.where(lane == 1, up_power, down_power))
    o_ref[:, 3 * hidden :] = powers


def hidden_kernel(hidden, p_ref, o_ref):
    def total(which):
        value = None
        for j in range(p_ref.shape[0]):
            at = 3 * hidden + which
            factor = jnp.exp2(p_ref[j, :, 3 * hidden :][:, which : which + 1])
            term = p_ref[j, :, which * hidden : (which + 1) * hidden] * factor
            value = term if value is None else value + term
        return value

    a, b, r = total(0), total(1), total(2)
    sig = jax.nn.sigmoid(a)
    silu = a * sig
    o_ref[:, :hidden] = (r * b * (sig * (1.0 + a * (1.0 - sig)))).astype(BF)
    o_ref[:, hidden : 2 * hidden] = (r * silu).astype(BF)
    route = jnp.sum(silu * b * r, axis=1, keepdims=True)
    hi = route.astype(BF).astype(F32)
    mid = (route - hi).astype(BF).astype(F32)
    lo = route - hi - mid
    lane = iota((route.shape[0], 128), 1)
    pieces = jnp.where(lane == 0, hi, jnp.where(lane == 1, mid, jnp.where(lane == 2, lo, 0.0)))
    o_ref[:, 2 * hidden :] = pieces.astype(BF)


def return_kernel(core_ref, d_ref, own_ref, other_hbm, o_ref, other_ref, sems):
    core = core_ref[0]
    hidden = own_ref.shape[0]
    width = own_ref.shape[1] - hidden
    copies = bring(other_hbm, other_ref, sems, weight_places(width, hidden)[:2])
    rows = d_ref.shape[0] * d_ref.shape[1]
    grads = d_ref[...].reshape(rows, -1)
    d_gate = grads[:, :hidden]
    d_up = grads[:, hidden : 2 * hidden]
    own = (dot_t(d_gate, own_ref[:width, width:]) + dot_t(d_up, own_ref[width:, width:])).astype(BF)
    for copy in copies:
        copy.wait()
    other = (
        dot_t(d_gate, other_ref[:width, width:]) + dot_t(d_up, other_ref[width:, width:])
    ).astype(BF)
    q = iota((2 * rows, rows), 0)
    here = (q // ROWS) * MOST + q % MOST == iota((2 * rows, rows), 1)
    mine = (q // MOST) % 2 == core
    to_own = (here & mine).astype(BF)
    to_other = (here & ~mine).astype(BF)
    o_ref[:, :width] = (dot(to_own, own) + dot(to_other, other)).astype(BF)
    o_ref[:, width:] = dot(here.astype(BF), grads[:, 2 * hidden :]).astype(BF)


def combine_kernel(hi_ref, lo_ref, pick_ref, b_ref, o_ref):
    toks, rows, _ = hi_ref.shape
    width = b_ref.shape[1] - 128
    value = b_ref[:, :width]
    extra = b_ref[:, width:]
    lane = iota((rows, 128), 1)
    routes = jnp.zeros((rows, 128), F32)
    for t in range(toks):
        total = dot(hi_ref[t], value) + dot(lo_ref[t], value)
        o_ref[:, t * width : (t + 1) * width] = total.astype(BF)
        route = jnp.sum(dot(pick_ref[t], extra), axis=1, keepdims=True)
        hi = route.astype(BF).astype(F32)
        routes = jnp.where(lane == 2 * t, hi, jnp.where(lane == 2 * t + 1, route - hi, routes))
    o_ref[:, toks * width :] = routes.astype(BF)


def home_kernel(toks, width, h_ref, x_ref, r_ref):
    total = h_ref[0].astype(F32)
    for g in range(1, h_ref.shape[0]):
        total = total + h_ref[g].astype(F32)
    top = r_ref.shape[2]
    extra = total[:, toks * width :]
    lane = iota(extra.shape, 1)
    diagonal = iota((SPLIT, top), 0) == iota((SPLIT, top), 1)
    for t in range(toks):
        for s in range(SPLIT):
            x_ref[t, :, s * width : (s + 1) * width] = total[
                s : s + 1, t * width : (t + 1) * width
            ]
        route = jnp.sum(jnp.where(lane // 2 == t, extra, 0.0), axis=1, keepdims=True)
        r_ref[t] = jnp.sum(jnp.where(diagonal, route, 0.0), axis=0, keepdims=True)


def body(grad_out, inputs, expert_ids, route_weights, w_gate, w_up, w_down):
    groups = lax.axis_size("z")
    chips_y = lax.axis_size("yl")
    experts = lax.axis_size("x") * lax.axis_size("yh")
    chips = experts * chips_y
    toks = grad_out.shape[1]
    width, hidden = w_gate.shape[1:]
    top = expert_ids.shape[2]
    core = lax.axis_index("c").astype(jnp.int32).reshape(1)
    first = (lax.axis_index("z") * experts).astype(jnp.int32).reshape(1)
    held = groups * SPLIT
    sent = chips * ROWS
    rows = chips * MOST

    swap = [(0, 1), (1, 0)]

    payload, weights = pl.pallas_call(
        functools.partial(start_kernel, toks),
        out_shape=[
            jax.ShapeDtypeStruct((SPLIT, 2 * toks * width), BF),
            jax.ShapeDtypeStruct((hidden, width + hidden), BF),
        ],
        in_specs=[pl.BlockSpec(memory_space=pltpu.HBM)] * 5,
        out_specs=[
            pl.BlockSpec(memory_space=pltpu.VMEM),
            pl.BlockSpec(memory_space=pltpu.HBM),
        ],
        scratch_shapes=[
            pltpu.VMEM((2,) + inputs.shape, BF),
            pltpu.VMEM((hidden, width + hidden), BF),
            pltpu.SemaphoreType.DMA((8,)),
        ],
        compiler_params=pltpu.CompilerParams(vmem_limit_bytes=60 << 20),
    )(inputs, grad_out, w_gate, w_up, w_down)
    other = lax.ppermute(weights, "c", swap)
    tokens = lax.all_gather(payload, "z", axis=0, tiled=False)

    pick = call(
        functools.partial(pick_kernel, toks, experts, chips_y),
        jax.ShapeDtypeStruct((toks, sent, held), BF),
        8,
        first,
        expert_ids[0].T,
        smem=1,
    )
    merged = jax.ShapeDtypeStruct((toks, held, sent), BF)
    merge_hi, merge_lo, merge_pick = call(
        functools.partial(merge_kernel, toks, experts, chips_y),
        [merged, merged, merged],
        8,
        first,
        expert_ids[0].T,
        route_weights[0].T,
        smem=1,
    )

    packed = call(pack_kernel, jax.ShapeDtypeStruct((sent, 2 * width), BF), 8, pick, tokens)
    got = lax.all_to_all(
        packed.reshape(chips, ROWS, 2 * width), CHIPS, split_axis=0, concat_axis=0, tiled=True
    ).reshape(sent, 2 * width)

    partials = call(
        partial_kernel,
        jax.ShapeDtypeStruct((rows, 3 * hidden + 128), F32),
        20,
        core,
        got,
        weights,
        other,
        smem=1,
        hbm=1,
        scratch=[pltpu.VMEM(weights.shape, BF), pltpu.SemaphoreType.DMA((3,))],
    )
    shares = partials.astype(jnp.float16).reshape(chips_y, rows // chips_y, -1)
    shares = lax.all_to_all(shares, "yl", split_axis=0, concat_axis=0, tiled=True)
    grads = call(
        functools.partial(hidden_kernel, hidden),
        jax.ShapeDtypeStruct((rows // chips_y, 2 * hidden + 128), BF),
        8,
        shares.astype(F32),
    )
    all_grads = lax.all_gather(grads, "yl", axis=0, tiled=False)

    back = call(
        return_kernel,
        jax.ShapeDtypeStruct((sent, width + 128), BF),
        20,
        core,
        all_grads,
        weights,
        other,
        smem=1,
        hbm=1,
        scratch=[pltpu.VMEM(weights.shape, BF), pltpu.SemaphoreType.DMA((3,))],
    )
    back = lax.all_to_all(
        back.reshape(chips, ROWS, -1), CHIPS, split_axis=0, concat_axis=0, tiled=True
    ).reshape(sent, -1)

    home = call(
        combine_kernel,
        jax.ShapeDtypeStruct((held, toks * width + 128), BF),
        8,
        merge_hi,
        merge_lo,
        merge_pick,
        back,
    )
    home = lax.all_to_all(
        home.reshape(groups, SPLIT, -1), "z", split_axis=0, concat_axis=0, tiled=True
    )
    grad_in, grad_route = call(
        functools.partial(home_kernel, toks, width),
        [
            jax.ShapeDtypeStruct((toks, 1, SPLIT * width), F32),
            jax.ShapeDtypeStruct((toks, 1, top), F32),
        ],
        8,
        home,
    )
    return jnp.swapaxes(grad_in, 0, 1), jnp.swapaxes(grad_route, 0, 1)


def solution(mesh):
    groups, members = mesh.devices.shape
    chips_y = SPLIT // 2
    x = 4 if members == 64 else 2
    fine = Mesh(
        mesh.devices.reshape(groups, x, members // (x * SPLIT), chips_y, 2), ("z",) + CORES
    )
    tokens = P(CORES, "z", None)
    tables = P(CORES, None, None)
    weights = P(("z",) + CORES, None, None)
    return jax.shard_map(
        body,
        mesh=fine,
        in_specs=(tokens, tokens, tables, tables, weights, weights, weights),
        out_specs=(tokens, tokens),
        check_vma=False,
    )
```

time: 171 us -> 164 us (0.959)
  local copies, waits for them, and re-layouts: 6.75 us -> 0.8 us
  Pallas kernels: 10 us -> 15.6 us
  blocking collectives: 105 us -> 101 us
  starting transfers between devices: 23.3 us -> 20.3 us
    unnamed x20 -> x8, local copies, waits for them, and re-layouts: 6.75 us -> 0.8 us
    all_gather x2, blocking collectives: 61.8 us -> 57.1 us  [the longest x1 43.8 us: body(): tokens = lax.all_gather(payload, 'z', axis=0, tiled=False)]
    ppermute x3 -> x1, starting transfers between devices: 6.26 us -> 2.18 us  [body(): other = lax.ppermute(weights, 'c', swap)]
    pallas_call x0 -> x1, Pallas kernels: none -> 3.66 us  [body(): pl.pallas_call(functools.partial(start_kernel, toks), out_shape=[jax.Shap...]
    all_to_all x1, blocking collectives: 23.6 us -> 25.9 us  [body(): lax.all_to_all(home.reshape(groups, SPLIT, -1), 'z', split_axis=0, concat...]
    pallas_call x9 -> x8, Pallas kernels: 10 us -> 12 us  [call(): pl.pallas_call(kernel, out_shape=out, in_specs=[pl.BlockSpec(memory_space...]
  transfers between devices with their start and end apart: 5 -> 3, of which waited for: 2 -> 2; matrix products, arithmetic and copies ran while one was open for 0% -> 0% of each run, Pallas kernels for 1% -> 1%
where the time goes in v2:
time: 164 us; the launch traced here: 163 us
  blocking collectives  101 us (62%)
  waiting for transfers between devices  24.4 us (15%)
  starting transfers between devices  20.3 us (12%)
  Pallas kernels  15.6 us (10%)
    all_gather x1, blocking collectives, body(): tokens = lax.all_gather(payload, 'z', axis=0, tiled=False)  43.8 us
    all_to_all x1, blocking collectives, body(): lax.all_to_all(home.reshape(groups, SPLIT, -1), 'z', split_axis=0, concat...  25.9 us
    all_to_all x1, blocking collectives, body(): lax.all_to_all(shares, 'yl', split_axis=0, concat_axis=0, tiled=True)  18 us
    all_to_all x1, waiting for transfers between devices, body(): lax.all_to_all(packed.reshape(chips, ROWS, 2 * width), CHIPS, split_axis=...  13.7 us
    all_gather x1, blocking collectives, body(): all_grads = lax.all_gather(grads, 'yl', axis=0, tiled=False)  13.3 us
    pallas_call x8, Pallas kernels, call(): pl.pallas_call(kernel, out_shape=out, in_specs=[pl.BlockSpec(memory_space...  12 us
    all_to_all x1, waiting for transfers between devices, body(): lax.all_to_all(back.reshape(chips, ROWS, -1), CHIPS, split_axis=0, concat...  10.7 us
    all_to_all x1, starting transfers between devices, body(): lax.all_to_all(packed.reshape(chips, ROWS, 2 * width), CHIPS, split_axis=...  10.2 us
  transfers between devices with their start and end apart: 3, of which 2 were waited for; matrix products, arithmetic and copies ran while one was open for 0% of the time, Pallas kernels for 1%

profile of v2, /device:TPU:72, one launch (start us, length us, event | category | flops | bytes accessed | tf_op | source)
XLA Modules:
  0.0 163.1 jit_solution(12571784171020449328)
XLA Ops:
  0.6 0.0 copy-start.2
  0.6 3.7 %shard_map.88 = (bf16[8,3072]{1,0:T(8,128)(2,1)}, bf16[1024,1536]{1,0:T(8,128)(2,1)}) custom-call(bf16[1,3,4096]{2,1,0:T(4,128)(2,1)} %x_hbm.1, bf16[1,3,4096]{2,1,0:T(4,128)(2,1)} %g_hbm.1, bf16[1,512,1024]{2,1,0:T(8,128)(2,1)} %wg_hbm.1, bf16[1,512,1024]{2,1,0:T(8,128)(2,1)} %wu_hbm.1, bf16[1,1024,512]{2,1,0:T(8,128)(2,1)} %wd_hbm.1), custom_call_target="tpu_custom_call" | custom-call | tf_op jit(solution)/shard_map/pallas_call | solution.py:321
  4.3 0.0 copy-start
  4.3 2.2 %collective-permute-start = (bf16[1024,1536]{1,0:T(8,128)(2,1)}, bf16[1024,1536]{1,0:T(8,128)(2,1)}, u32[]{:S(2)}, u32[]{:S(2)}) collective-permute-start(bf16[1024,1536]{1,0:T(8,128)(2,1)} %get-tuple-element.13.own_ref), channel_id=1, source_target_pairs={{0,1},{1,0},{2,3},{3,2},{4,5},{5,4},{6,7},{7,6},{8,9},{9,8},{10,11... | collective-permute-start | bytes 9437192 | tf_op jit(solution)/shard_map/ppermute | solution.py:339
  6.5 0.0 copy-done.2
  6.5 0.4 shard_map.87.pick_ref
  7.0 43.8 %all-gather = bf16[128,3072]{1,0:T(8,128)(2,1)S(1)} all-gather(bf16[8,3072]{1,0:T(8,128)(2,1)} %get-tuple-element.12), channel_id=2, replica_groups=mesh['z'=16,'x'=4,'yh'=2,'yl'=4,'c'=2] {'z'}, dimensions={0}, use_global_device_ids=true | all-gather | bytes 835584 | tf_op jit(solution)/shard_map/all_gather | solution.py:340
  50.8 0.5 shard_map.89
  51.4 0.0 copy-start.1
  51.4 0.8 copy-done.1
  52.2 10.2 %all-to-all-start = ((bf16[32,8,1024]{2,1,0:T(8,128)(2,1)}), bf16[32,8,1024]{2,1,0:T(8,128)(2,1)}, u32[]{:S(2)}, u32[]{:S(2)}) async-start(bf16[32,8,1024]{2,1,0:T(8,128)(2,1)} %bitcast.20), calls=%async_computation | async-start | bytes 1048576 | tf_op jit(solution)/shard_map/all_to_all | solution.py:362
  62.4 13.7 %all-to-all-done = bf16[32,8,1024]{2,1,0:T(8,128)(2,1)} async-done(((bf16[32,8,1024]{2,1,0:T(8,128)(2,1)}), bf16[32,8,1024]{2,1,0:T(8,128)(2,1)}, u32[]{:S(2)}, u32[]{:S(2)}) %all-to-all-start) | async-done | bytes 524320 | tf_op jit(solution)/shard_map/all_to_all | solution.py:362
  76.1 0.0 collective-permute-done.other_hbm
  76.1 0.0 copy-done
  76.1 4.5 %shard_map.90 = f32[128,3200]{1,0:T(8,128)S(1)} custom-call(s32[1]{0:T(128)} %bitcast.5.core_ref, bf16[256,1024]{1,0:T(8,128)(2,1)} %bitcast.9.rows_ref, bf16[1024,1536]{1,0:T(8,128)(2,1)S(1)} %copy-done, bf16[1024,1536]{1,0:T(8,128)(2,1)} %collective-permute-done.other_hbm), custom_call_target="tpu_custom_call" | custom-call | tf_op jit(solution)/shard_map/pallas_call | solution.py:37
  80.6 0.1 convert_element_type.6
  80.7 18.0 %all_to_all.20 = f16[4,32,3200]{2,1,0:T(8,128)(2,1)S(1)} all-to-all(f16[4,32,3200]{2,1,0:T(8,128)(2,1)S(1)} %bitcast.26), channel_id=1, replica_groups=mesh['z'=16,'x'=4,'yh'=2,'yl'=4,'c'=2] {'yl'}, dimensions={0} | all-to-all | bytes 1638400 | tf_op jit(solution)/shard_map/all_to_all | solution.py:379
  98.6 0.1 convert_element_type.7.p_ref
  98.7 0.3 shard_map.91
  99.0 13.3 %all-gather.1 = bf16[128,2176]{1,0:T(8,128)(2,1)S(1)} all-gather(bf16[32,2176]{1,0:T(8,128)(2,1)S(1)} %shard_map.91), channel_id=3, replica_groups=mesh['z'=16,'x'=4,'yh'=2,'yl'=4,'c'=2] {'yl'}, dimensions={0}, use_global_device_ids=true | all-gather | bytes 696320 | tf_op jit(solution)/shard_map/all_gather | solution.py:386
  112.3 0.0 copy-start.3
  112.3 4.1 %shard_map.92 = bf16[256,640]{1,0:T(8,128)(2,1)} custom-call(s32[1]{0:T(128)} %bitcast.5.core_ref, bf16[4,32,2176]{2,1,0:T(8,128)(2,1)S(1)} %bitcast.19, bf16[1024,1536]{1,0:T(8,128)(2,1)S(1)} %copy-done, bf16[1024,1536]{1,0:T(8,128)(2,1)} %collective-permute-done.other_hbm), custom_call_target="tpu_custom_call" | custom-call | tf_op jit(solution)/shard_map/pallas_call | solution.py:37
  116.4 7.9 %all-to-all-start.2 = ((bf16[32,8,640]{2,1,0:T(8,128)(2,1)}), bf16[32,8,640]{2,1,0:T(8,128)(2,1)S(1)}, u32[]{:S(2)}, u32[]{:S(2)}) async-start(bf16[32,8,640]{2,1,0:T(8,128)(2,1)} %bitcast.12), calls=%async_computation.2 | async-start | bytes 655360 | tf_op jit(solution)/shard_map/all_to_all | solution.py:400
  124.3 0.0 copy-done.3
  124.3 0.9 shard_map.86
  125.3 10.7 %all-to-all-done.2 = bf16[32,8,640]{2,1,0:T(8,128)(2,1)S(1)} async-done(((bf16[32,8,640]{2,1,0:T(8,128)(2,1)}), bf16[32,8,640]{2,1,0:T(8,128)(2,1)S(1)}, u32[]{:S(2)}, u32[]{:S(2)}) %all-to-all-start.2) | async-done | bytes 327712 | tf_op jit(solution)/shard_map/all_to_all | solution.py:400
  136.0 0.5 shard_map.93
  136.5 25.9 %all_to_all.21.h_ref = bf16[16,8,1664]{2,1,0:T(8,128)(2,1)S(1)} all-to-all(bf16[16,8,1664]{2,1,0:T(8,128)(2,1)S(1)} %bitcast.21), channel_id=1, replica_groups=mesh['z'=16,'x'=4,'yh'=2,'yl'=4,'c'=2] {'z'}, dimensions={0} | all-to-all | bytes 851968 | tf_op jit(solution)/shard_map/all_to_all | solution.py:413
  162.4 0.7 shard_map.94
Async XLA Ops:
  0.6 5.9 %copy-start.2 = (s32[1,48,8]{1,2,0:T(8,128)S(1)}, s32[1,48,8]{1,2,0:T(8,128)}, u32[]{:S(2)}) copy-start(s32[1,48,8]{1,2,0:T(8,128)} %param.9) | copy-start | bytes 4612
  4.3 71.8 %copy-start = (bf16[1024,1536]{1,0:T(8,128)(2,1)S(1)}, bf16[1024,1536]{1,0:T(8,128)(2,1)}, u32[]{:S(2)}) copy-start(bf16[1024,1536]{1,0:T(8,128)(2,1)} %get-tuple-element.13.own_ref) | copy-start | bytes 9437188
  4.3 71.7 %collective-permute-start = (bf16[1024,1536]{1,0:T(8,128)(2,1)}, bf16[1024,1536]{1,0:T(8,128)(2,1)}, u32[]{:S(2)}, u32[]{:S(2)}) collective-permute-start(bf16[1024,1536]{1,0:T(8,128)(2,1)} %get-tuple-element.13.own_ref), channel_id=1, source_target_pairs={{0,1},{1,0},{2,3},{3,2},{4,5},{5,4},{6,7},{7,6},{8,9},{9,8},{10,11... | collective-permute-start | bytes 9437192 | tf_op jit(solution)/shard_map/ppermute | solution.py:339
  51.4 0.8 copy-start.1
  52.2 23.9 %all-to-all-start = ((bf16[32,8,1024]{2,1,0:T(8,128)(2,1)}), bf16[32,8,1024]{2,1,0:T(8,128)(2,1)}, u32[]{:S(2)}, u32[]{:S(2)}) async-start(bf16[32,8,1024]{2,1,0:T(8,128)(2,1)} %bitcast.20), calls=%async_computation | async-start | bytes 1048576 | tf_op jit(solution)/shard_map/all_to_all | solution.py:362
  112.3 12.0 %copy-start.3 = (f32[1,48,8]{1,2,0:T(8,128)S(1)}, f32[1,48,8]{1,2,0:T(8,128)}, u32[]{:S(2)}) copy-start(f32[1,48,8]{1,2,0:T(8,128)} %param.10) | copy-start | bytes 4612
  116.4 19.6 %all-to-all-start.2 = ((bf16[32,8,640]{2,1,0:T(8,128)(2,1)}), bf16[32,8,640]{2,1,0:T(8,128)(2,1)S(1)}, u32[]{:S(2)}, u32[]{:S(2)}) async-start(bf16[32,8,640]{2,1,0:T(8,128)(2,1)} %bitcast.12), calls=%async_computation.2 | async-start | bytes 655360 | tf_op jit(solution)/shard_map/all_to_all | solution.py:400

commit v3 on v2

--- a/solution.py
+++ b/solution.py
@@ -29,9 +29,8 @@
     return lax.broadcasted_iota(jnp.int32, shape, axis)
 
 
-def call(kernel, out, limit_mib, *args, smem=0, hbm=0, scratch=()):
-    inside = len(args) - smem - hbm
-    spaces = [pltpu.SMEM] * smem + [pltpu.VMEM] * inside + [pltpu.HBM] * hbm
+def call(kernel, out, limit_mib, *args, smem=0):
+    spaces = [pltpu.SMEM] * smem + [pltpu.VMEM] * (len(args) - smem)
     many = isinstance(out, (list, tuple))
     outs = [pl.BlockSpec(memory_space=pltpu.VMEM) for _ in out] if many else None
     return pl.pallas_call(
@@ -39,44 +38,15 @@
         out_shape=out,
         in_specs=[pl.BlockSpec(memory_space=space) for space in spaces],
         out_specs=outs if many else pl.BlockSpec(memory_space=pltpu.VMEM),
-        scratch_shapes=scratch,
         compiler_params=pltpu.CompilerParams(vmem_limit_bytes=limit_mib << 20),
     )(*args)
 
 
-def weight_places(width, hidden):
-    return (
-        (pl.ds(0, width), pl.ds(width, hidden)),
-        (pl.ds(width, width), pl.ds(width, hidden)),
-        (pl.ds(0, hidden), pl.ds(0, width)),
-    )
-
-
-def bring(source, room, sems, places):
-    copies = [
-        pltpu.make_async_copy(source.at[place], room.at[place], sems.at[i])
-        for i, place in enumerate(places)
-    ]
-    for copy in copies:
-        copy.start()
-    return copies
-
-
-def start_kernel(toks, x_hbm, g_hbm, wg_hbm, wu_hbm, wd_hbm, o_ref, all_hbm, held, room, sems):
-    width, hidden = wg_hbm.shape[1:]
+def payload_kernel(toks, width, x_hbm, g_hbm, o_ref, held, sems):
     copies = [
         pltpu.make_async_copy(ref, held.at[i], sems.at[i]) for i, ref in enumerate((x_hbm, g_hbm))
     ]
-    moves = [
-        (
-            pltpu.make_async_copy(ref.at[0], room.at[place], sems.at[2 + i]),
-            pltpu.make_async_copy(room.at[place], all_hbm.at[place], sems.at[5 + i]),
-        )
-        for i, (ref, place) in enumerate(
-            zip((wg_hbm, wu_hbm, wd_hbm), weight_places(width, hidden))
-        )
-    ]
-    for copy in copies + [come for come, _ in moves]:
+    for copy in copies:
         copy.start()
     for tensor, copy in enumerate(copies):
         copy.wait()
@@ -85,11 +55,6 @@
             rows = [value[t : t + 1, s * width : (s + 1) * width] for s in range(SPLIT)]
             at = (t * 2 + tensor) * width
             o_ref[:, at : at + width] = jnp.concatenate(rows, axis=0).astype(BF)
-    for come, go in moves:
-        come.wait()
-        go.start()
-    for _, go in moves:
-        go.wait()
 
 
 def spread_rows(rows):
@@ -119,10 +84,10 @@
     return index // (MOST * 2 * chips_y), part, slot
 
 
-def pick_kernel(toks, experts, chips_y, first_ref, ids_ref, o_ref):
+def pick_kernel(toks, experts, chips_y, place_ref, ids_ref, o_ref):
     _, rows, lanes = o_ref.shape
     column = ids_ref.shape[1]
-    rank = rank_table(ids_ref[...], first_ref[0], experts).astype(BF)
+    rank = rank_table(ids_ref[...], place_ref[0], experts).astype(BF)
     expert, _, _ = row_fields(iota((rows, experts), 0), chips_y)
     spread = dot((expert == iota((rows, experts), 1)).astype(BF), rank).astype(BF)
     _, part, slot = row_fields(iota((rows, lanes), 0), chips_y)
@@ -134,11 +99,11 @@
         o_ref[t] = (same_part & (table == slot.astype(F32))).astype(BF)
 
 
-def merge_kernel(toks, experts, chips_y, first_ref, ids_ref, w_ref, hi_ref, lo_ref, pick_ref):
+def merge_kernel(toks, experts, chips_y, place_ref, ids_ref, w_ref, hi_ref, lo_ref, pick_ref):
     _, rows, lanes = hi_ref.shape
     column = ids_ref.shape[1]
     ids = ids_ref[...]
-    first = first_ref[0]
+    first = place_ref[0]
     rank = rank_table(ids, first, experts).astype(BF)
     weights = w_ref[...]
     scale = spread_rows(
@@ -188,13 +153,11 @@
     return value * jnp.exp2(-power), power
 
 
-def partial_kernel(core_ref, rows_ref, own_ref, other_hbm, o_ref, other_ref, sems):
-    core = core_ref[0]
+def partial_kernel(place_ref, rows_ref, own_ref, other_ref, o_ref):
+    core = place_ref[1]
     both = rows_ref.shape[0]
     hidden = own_ref.shape[0]
     width = own_ref.shape[1] - hidden
-    places = weight_places(width, hidden)
-    copies = bring(other_hbm, other_ref, sems, places)
     rows = both // 2
     q = iota((both, both), 0)
     half = jnp.where(q < rows, core, 1 - core)
@@ -207,13 +170,10 @@
     gate = dot(x_own, own_ref[:width, width:])
     up = dot(x_own, own_ref[width:, width:])
     down = dot_t(g_own, own_ref[:, :width])
-    copies[0].wait()
     gate, gate_power = scaled(gate + dot(x_other, other_ref[:width, width:]))
     o_ref[:, :hidden] = gate
-    copies[1].wait()
     up, up_power = scaled(up + dot(x_other, other_ref[width:, width:]))
     o_ref[:, hidden : 2 * hidden] = up
-    copies[2].wait()
     down, down_power = scaled(down + dot_t(g_other, other_ref[:, :width]))
     o_ref[:, 2 * hidden : 3 * hidden] = down
     lane = iota((rows, 128), 1)
@@ -245,18 +205,15 @@
     o_ref[:, 2 * hidden :] = pieces.astype(BF)
 
 
-def return_kernel(core_ref, d_ref, own_ref, other_hbm, o_ref, other_ref, sems):
-    core = core_ref[0]
+def return_kernel(place_ref, d_ref, own_ref, other_ref, o_ref):
+    core = place_ref[1]
     hidden = own_ref.shape[0]
     width = own_ref.shape[1] - hidden
-    copies = bring(other_hbm, other_ref, sems, weight_places(width, hidden)[:2])
     rows = d_ref.shape[0] * d_ref.shape[1]
     grads = d_ref[...].reshape(rows, -1)
     d_gate = grads[:, :hidden]
     d_up = grads[:, hidden : 2 * hidden]
     own = (dot_t(d_gate, own_ref[:width, width:]) + dot_t(d_up, own_ref[width:, width:])).astype(BF)
-    for copy in copies:
-        copy.wait()
     other = (
         dot_t(d_gate, other_ref[:width, width:]) + dot_t(d_up, other_ref[width:, width:])
     ).astype(BF)
@@ -310,32 +267,26 @@
     toks = grad_out.shape[1]
     width, hidden = w_gate.shape[1:]
     top = expert_ids.shape[2]
-    core = lax.axis_index("c").astype(jnp.int32).reshape(1)
-    first = (lax.axis_index("z") * experts).astype(jnp.int32).reshape(1)
+    place = jnp.stack([lax.axis_index("z") * experts, lax.axis_index("c")]).astype(jnp.int32)
     held = groups * SPLIT
     sent = chips * ROWS
     rows = chips * MOST
 
     swap = [(0, 1), (1, 0)]
 
-    payload, weights = pl.pallas_call(
-        functools.partial(start_kernel, toks),
-        out_shape=[
-            jax.ShapeDtypeStruct((SPLIT, 2 * toks * width), BF),
-            jax.ShapeDtypeStruct((hidden, width + hidden), BF),
-        ],
-        in_specs=[pl.BlockSpec(memory_space=pltpu.HBM)] * 5,
-        out_specs=[
-            pl.BlockSpec(memory_space=pltpu.VMEM),
-            pl.BlockSpec(memory_space=pltpu.HBM),
-        ],
+    place, down = lax.optimization_barrier((place, w_down[0]))
+    weights = jnp.concatenate([down, jnp.concatenate([w_gate[0], w_up[0]], axis=0)], axis=1)
+    payload = pl.pallas_call(
+        functools.partial(payload_kernel, toks, width),
+        out_shape=jax.ShapeDtypeStruct((SPLIT, 2 * toks * width), BF),
+        in_specs=[pl.BlockSpec(memory_space=pltpu.HBM)] * 2,
+        out_specs=pl.BlockSpec(memory_space=pltpu.VMEM),
         scratch_shapes=[
             pltpu.VMEM((2,) + inputs.shape, BF),
-            pltpu.VMEM((hidden, width + hidden), BF),
-            pltpu.SemaphoreType.DMA((8,)),
+            pltpu.SemaphoreType.DMA((2,)),
         ],
-        compiler_params=pltpu.CompilerParams(vmem_limit_bytes=60 << 20),
-    )(inputs, grad_out, w_gate, w_up, w_down)
+        compiler_params=pltpu.CompilerParams(vmem_limit_bytes=4 << 20),
+    )(inputs, grad_out)
     other = lax.ppermute(weights, "c", swap)
     tokens = lax.all_gather(payload, "z", axis=0, tiled=False)
 
@@ -343,7 +294,7 @@
         functools.partial(pick_kernel, toks, experts, chips_y),
         jax.ShapeDtypeStruct((toks, sent, held), BF),
         8,
-        first,
+        place,
         expert_ids[0].T,
         smem=1,
     )
@@ -352,7 +303,7 @@
         functools.partial(merge_kernel, toks, experts, chips_y),
         [merged, merged, merged],
         8,
-        first,
+        place,
         expert_ids[0].T,
         route_weights[0].T,
         smem=1,
@@ -367,13 +318,11 @@
         partial_kernel,
         jax.ShapeDtypeStruct((rows, 3 * hidden + 128), F32),
         20,
-        core,
+        place,
         got,
         weights,
         other,
         smem=1,
-        hbm=1,
-        scratch=[pltpu.VMEM(weights.shape, BF), pltpu.SemaphoreType.DMA((3,))],
     )
     shares = partials.astype(jnp.float16).reshape(chips_y, rows // chips_y, -1)
     shares = lax.all_to_all(shares, "yl", split_axis=0, concat_axis=0, tiled=True)
@@ -389,13 +338,11 @@
         return_kernel,
         jax.ShapeDtypeStruct((sent, width + 128), BF),
         20,
-        core,
+        place,
         all_grads,
         weights,
         other,
         smem=1,
-        hbm=1,
-        scratch=[pltpu.VMEM(weights.shape, BF), pltpu.SemaphoreType.DMA((3,))],
     )
     back = lax.all_to_all(
         back.reshape(chips, ROWS, -1), CHIPS, split_axis=0, concat_axis=0, tiled=True

time: 164 us -> 158 us (0.963)
  blocking collectives: 101 us -> 125 us
  waiting for transfers between devices: 24.4 us -> 10.2 us
  starting transfers between devices: 20.3 us -> 9.94 us
  Pallas kernels: 15.6 us -> 9.96 us
  other arithmetic: 0.19 us -> 2.35 us
    all_to_all x0 -> x1, blocking collectives: none -> 23.6 us  [body(): lax.all_to_all(packed.reshape(chips, ROWS, 2 * width), CHIPS, split_axis=...]
    all_to_all x1 -> x0, waiting for transfers between devices: 13.7 us -> none  [body(): lax.all_to_all(packed.reshape(chips, ROWS, 2 * width), CHIPS, split_axis=...]
    all_to_all x1 -> x0, starting transfers between devices: 10.2 us -> none  [body(): lax.all_to_all(packed.reshape(chips, ROWS, 2 * width), CHIPS, split_axis=...]
    pallas_call x1, Pallas kernels: 3.66 us -> 0.17 us  [body(): pl.pallas_call(functools.partial(payload_kernel, toks, width), out_shape=...]
    pallas_call x8, Pallas kernels: 12 us -> 9.8 us  [call(): pl.pallas_call(kernel, out_shape=out, in_specs=[pl.BlockSpec(memory_space...]
    concatenate x0 -> x1, other arithmetic: none -> 2.08 us  [body(): jnp.concatenate([down, jnp.concatenate([w_gate[0], w_up[0]], axis=0)], ax...]
  transfers between devices with their start and end apart: 3 -> 2, of which waited for: 2 -> 1; matrix products, arithmetic and copies ran while one was open for 0% -> 0% of each run, Pallas kernels for 1% -> 2%
where the time goes in v3:
time: 158 us
  blocking collectives  125 us (79%)
  waiting for transfers between devices  10.2 us (6%)
  Pallas kernels  9.96 us (6%)
  starting transfers between devices  9.94 us (6%)
  other arithmetic  2.35 us (1%)
    all_gather x1, blocking collectives, body(): tokens = lax.all_gather(payload, 'z', axis=0, tiled=False)  43.7 us
    all_to_all x1, blocking collectives, body(): lax.all_to_all(home.reshape(groups, SPLIT, -1), 'z', split_axis=0, concat...  26.5 us
    all_to_all x1, blocking collectives, body(): lax.all_to_all(packed.reshape(chips, ROWS, 2 * width), CHIPS, split_axis=...  23.6 us
    all_to_all x1, blocking collectives, body(): lax.all_to_all(shares, 'yl', split_axis=0, concat_axis=0, tiled=True)  18 us
    all_gather x1, blocking collectives, body(): all_grads = lax.all_gather(grads, 'yl', axis=0, tiled=False)  13.2 us
    all_to_all x1, waiting for transfers between devices, body(): lax.all_to_all(back.reshape(chips, ROWS, -1), CHIPS, split_axis=0, concat...  10.2 us
    pallas_call x8, Pallas kernels, call(): pl.pallas_call(kernel, out_shape=out, in_specs=[pl.BlockSpec(memory_space...  9.8 us
    all_to_all x1, starting transfers between devices, body(): lax.all_to_all(back.reshape(chips, ROWS, -1), CHIPS, split_axis=0, concat...  8.02 us
  transfers between devices with their start and end apart: 2, of which 1 were waited for; matrix products, arithmetic and copies ran while one was open for 0% of the time, Pallas kernels for 2%

profile of v3, /device:TPU:72, one launch (start us, length us, event | category | flops | bytes accessed | tf_op | source)
XLA Modules:
  0.0 158.1 jit_solution(1308501053145440039)
XLA Ops:
  0.6 0.1 pad_add_fusion.place_ref
  0.7 0.0 copy-start.2
  0.7 0.0 copy-start
  0.7 0.0 copy-start.1
  0.7 2.1 %maximum_maximum_fusion.own_ref = bf16[1024,1536]{1,0:T(8,128)(2,1)S(1)} fusion(bf16[512,1024]{1,0:T(8,128)(2,1)} %bitcast.31, bf16[512,1024]{1,0:T(8,128)(2,1)} %bitcast.32, bf16[1024,512]{1,0:T(8,128)(2,1)} %bitcast.33), kind=kLoop, calls=%fused_computation | loop fusion | flops 9437184 | bytes 6291456 | tf_op jit(solution)/shard_map/concatenate | solution.py:278
  2.8 1.9 %collective-permute-start = (bf16[1024,1536]{1,0:T(8,128)(2,1)S(1)}, bf16[1024,1536]{1,0:T(8,128)(2,1)S(1)}, u32[]{:S(2)}, u32[]{:S(2)}) collective-permute-start(bf16[1024,1536]{1,0:T(8,128)(2,1)S(1)} %maximum_maximum_fusion.own_ref), channel_id=1, source_target_pairs={{0,1},{1,0},{2,3},{3,2},{4,5},{5,4},{6,7},{7,6},{8,9},{9,8},{10,11... | collective-permute-start | bytes 9437192 | tf_op jit(solution)/shard_map/ppermute | solution.py:290
  4.7 0.0 copy-done.2
  4.7 1.0 shard_map.87.pick_ref
  5.7 0.0 copy-done
  5.7 0.0 copy-done.1
  5.8 0.2 shard_map.88
  5.9 43.7 %all-gather = bf16[128,3072]{1,0:T(8,128)(2,1)S(1)} all-gather(bf16[8,3072]{1,0:T(8,128)(2,1)S(1)} %shard_map.88), channel_id=2, replica_groups=mesh['z'=16,'x'=4,'yh'=2,'yl'=4,'c'=2] {'z'}, dimensions={0}, use_global_device_ids=true | all-gather | bytes 835584 | tf_op jit(solution)/shard_map/all_gather | solution.py:291
  49.6 0.6 shard_map.89
  50.2 23.6 %all_to_all.20 = bf16[32,8,1024]{2,1,0:T(8,128)(2,1)S(1)} all-to-all(bf16[32,8,1024]{2,1,0:T(8,128)(2,1)S(1)} %bitcast.24), channel_id=1, replica_groups=mesh['z'=16,'x'=4,'yh'=2,'yl'=4,'c'=2] {'x','yh','yl'}, dimensions={0} | all-to-all | bytes 1048576 | tf_op jit(solution)/shard_map/all_to_all | solution.py:313
  73.7 0.0 collective-permute-done.other_ref
  73.7 2.2 %shard_map.90 = f32[128,3200]{1,0:T(8,128)S(1)} custom-call(s32[2]{0:T(128)S(1)} %pad_add_fusion.place_ref, bf16[256,1024]{1,0:T(8,128)(2,1)S(1)} %bitcast.23, bf16[1024,1536]{1,0:T(8,128)(2,1)S(1)} %maximum_maximum_fusion.own_ref, bf16[1024,1536]{1,0:T(8,128)(2,1)S(1)} %collective-permute-done.other_ref), custom_call_target="tpu_custom_call" | custom-call | tf_op jit(solution)/shard_map/pallas_call | solution.py:36
  76.0 0.1 convert_element_type.6
  76.1 18.0 %all_to_all.21 = f16[4,32,3200]{2,1,0:T(8,128)(2,1)S(1)} all-to-all(f16[4,32,3200]{2,1,0:T(8,128)(2,1)S(1)} %bitcast.30), channel_id=1, replica_groups=mesh['z'=16,'x'=4,'yh'=2,'yl'=4,'c'=2] {'yl'}, dimensions={0} | all-to-all | bytes 1638400 | tf_op jit(solution)/shard_map/all_to_all | solution.py:328
  94.1 0.1 convert_element_type.7.p_ref
  94.2 0.3 shard_map.91
  94.5 13.2 %all-gather.1 = bf16[128,2176]{1,0:T(8,128)(2,1)S(1)} all-gather(bf16[32,2176]{1,0:T(8,128)(2,1)S(1)} %shard_map.91), channel_id=3, replica_groups=mesh['z'=16,'x'=4,'yh'=2,'yl'=4,'c'=2] {'yl'}, dimensions={0}, use_global_device_ids=true | all-gather | bytes 696320 | tf_op jit(solution)/shard_map/all_gather | solution.py:335
  107.6 0.0 copy-start.3
  107.6 3.0 %shard_map.92 = bf16[256,640]{1,0:T(8,128)(2,1)} custom-call(s32[2]{0:T(128)S(1)} %pad_add_fusion.place_ref, bf16[4,32,2176]{2,1,0:T(8,128)(2,1)S(1)} %bitcast.22, bf16[1024,1536]{1,0:T(8,128)(2,1)S(1)} %maximum_maximum_fusion.own_ref, bf16[1024,1536]{1,0:T(8,128)(2,1)S(1)} %collective-permute-done.other_ref), custom_call_target="tpu_custom_call" | custom-call | tf_op jit(solution)/shard_map/pallas_call | solution.py:36
  110.7 8.0 %all-to-all-start.2 = ((bf16[32,8,640]{2,1,0:T(8,128)(2,1)}), bf16[32,8,640]{2,1,0:T(8,128)(2,1)S(1)}, u32[]{:S(2)}, u32[]{:S(2)}) async-start(bf16[32,8,640]{2,1,0:T(8,128)(2,1)} %bitcast.15), calls=%async_computation.2 | async-start | bytes 655360 | tf_op jit(solution)/shard_map/all_to_all | solution.py:347
  118.7 0.0 copy-done.3
  118.7 1.5 shard_map.86
  120.2 10.2 %all-to-all-done.2 = bf16[32,8,640]{2,1,0:T(8,128)(2,1)S(1)} async-done(((bf16[32,8,640]{2,1,0:T(8,128)(2,1)}), bf16[32,8,640]{2,1,0:T(8,128)(2,1)S(1)}, u32[]{:S(2)}, u32[]{:S(2)}) %all-to-all-start.2) | async-done | bytes 327712 | tf_op jit(solution)/shard_map/all_to_all | solution.py:347
  130.4 0.5 shard_map.93
  130.9 26.5 %all_to_all.22.h_ref = bf16[16,8,1664]{2,1,0:T(8,128)(2,1)S(1)} all-to-all(bf16[16,8,1664]{2,1,0:T(8,128)(2,1)S(1)} %bitcast.25), channel_id=1, replica_groups=mesh['z'=16,'x'=4,'yh'=2,'yl'=4,'c'=2] {'z'}, dimensions={0} | all-to-all | bytes 851968 | tf_op jit(solution)/shard_map/all_to_all | solution.py:360
  157.4 0.7 shard_map.94
Async XLA Ops:
  0.7 4.0 %copy-start.2 = (s32[1,48,8]{1,2,0:T(8,128)S(1)}, s32[1,48,8]{1,2,0:T(8,128)}, u32[]{:S(2)}) copy-start(s32[1,48,8]{1,2,0:T(8,128)} %param.9) | copy-start | bytes 4612
  0.7 5.0 %copy-start = (bf16[1,3,4096]{2,1,0:T(4,128)(2,1)S(1)}, bf16[1,3,4096]{2,1,0:T(4,128)(2,1)}, u32[]{:S(2)}) copy-start(bf16[1,3,4096]{2,1,0:T(4,128)(2,1)} %x_hbm.1) | copy-start | bytes 73732
  0.7 5.0 %copy-start.1 = (bf16[1,3,4096]{2,1,0:T(4,128)(2,1)S(1)}, bf16[1,3,4096]{2,1,0:T(4,128)(2,1)}, u32[]{:S(2)}) copy-start(bf16[1,3,4096]{2,1,0:T(4,128)(2,1)} %g_hbm.1) | copy-start | bytes 73732
  2.8 70.9 %collective-permute-start = (bf16[1024,1536]{1,0:T(8,128)(2,1)S(1)}, bf16[1024,1536]{1,0:T(8,128)(2,1)S(1)}, u32[]{:S(2)}, u32[]{:S(2)}) collective-permute-start(bf16[1024,1536]{1,0:T(8,128)(2,1)S(1)} %maximum_maximum_fusion.own_ref), channel_id=1, source_target_pairs={{0,1},{1,0},{2,3},{3,2},{4,5},{5,4},{6,7},{7,6},{8,9},{9,8},{10,11... | collective-permute-start | bytes 9437192 | tf_op jit(solution)/shard_map/ppermute | solution.py:290
  107.6 11.1 %copy-start.3 = (f32[1,48,8]{1,2,0:T(8,128)S(1)}, f32[1,48,8]{1,2,0:T(8,128)}, u32[]{:S(2)}) copy-start(f32[1,48,8]{1,2,0:T(8,128)} %param.10) | copy-start | bytes 4612
  110.7 19.7 %all-to-all-start.2 = ((bf16[32,8,640]{2,1,0:T(8,128)(2,1)}), bf16[32,8,640]{2,1,0:T(8,128)(2,1)S(1)}, u32[]{:S(2)}, u32[]{:S(2)}) async-start(bf16[32,8,640]{2,1,0:T(8,128)(2,1)} %bitcast.15), calls=%async_computation.2 | async-start | bytes 655360 | tf_op jit(solution)/shard_map/all_to_all | solution.py:347

commit v4 on v3

--- a/solution.py
+++ b/solution.py
@@ -29,14 +29,13 @@
     return lax.broadcasted_iota(jnp.int32, shape, axis)
 
 
-def call(kernel, out, limit_mib, *args, smem=0):
-    spaces = [pltpu.SMEM] * smem + [pltpu.VMEM] * (len(args) - smem)
+def call(kernel, out, limit_mib, *args):
     many = isinstance(out, (list, tuple))
     outs = [pl.BlockSpec(memory_space=pltpu.VMEM) for _ in out] if many else None
     return pl.pallas_call(
         kernel,
         out_shape=out,
-        in_specs=[pl.BlockSpec(memory_space=space) for space in spaces],
+        in_specs=[pl.BlockSpec(memory_space=pltpu.VMEM) for _ in args],
         out_specs=outs if many else pl.BlockSpec(memory_space=pltpu.VMEM),
         compiler_params=pltpu.CompilerParams(vmem_limit_bytes=limit_mib << 20),
     )(*args)
@@ -84,10 +83,10 @@
     return index // (MOST * 2 * chips_y), part, slot
 
 
-def pick_kernel(toks, experts, chips_y, place_ref, ids_ref, o_ref):
+def pick_kernel(toks, experts, chips_y, ids_ref, o_ref):
     _, rows, lanes = o_ref.shape
     column = ids_ref.shape[1]
-    rank = rank_table(ids_ref[...], place_ref[0], experts).astype(BF)
+    rank = rank_table(ids_ref[...], lax.axis_index("z") * experts, experts).astype(BF)
     expert, _, _ = row_fields(iota((rows, experts), 0), chips_y)
     spread = dot((expert == iota((rows, experts), 1)).astype(BF), rank).astype(BF)
     _, part, slot = row_fields(iota((rows, lanes), 0), chips_y)
@@ -99,11 +98,11 @@
         o_ref[t] = (same_part & (table == slot.astype(F32))).astype(BF)
 
 
-def merge_kernel(toks, experts, chips_y, place_ref, ids_ref, w_ref, hi_ref, lo_ref, pick_ref):
+def merge_kernel(toks, experts, chips_y, ids_ref, w_ref, hi_ref, lo_ref, pick_ref):
     _, rows, lanes = hi_ref.shape
     column = ids_ref.shape[1]
     ids = ids_ref[...]
-    first = place_ref[0]
+    first = lax.axis_index("z") * experts
     rank = rank_table(ids, first, experts).astype(BF)
     weights = w_ref[...]
     scale = spread_rows(
@@ -153,8 +152,8 @@
     return value * jnp.exp2(-power), power
 
 
-def partial_kernel(place_ref, rows_ref, own_ref, other_ref, o_ref):
-    core = place_ref[1]
+def partial_kernel(rows_ref, own_ref, other_ref, o_ref):
+    core = lax.axis_index("c")
     both = rows_ref.shape[0]
     hidden = own_ref.shape[0]
     width = own_ref.shape[1] - hidden
@@ -205,8 +204,8 @@
     o_ref[:, 2 * hidden :] = pieces.astype(BF)
 
 
-def return_kernel(place_ref, d_ref, own_ref, other_ref, o_ref):
-    core = place_ref[1]
+def return_kernel(d_ref, own_ref, other_ref, o_ref):
+    core = lax.axis_index("c")
     hidden = own_ref.shape[0]
     width = own_ref.shape[1] - hidden
     rows = d_ref.shape[0] * d_ref.shape[1]
@@ -267,15 +266,13 @@
     toks = grad_out.shape[1]
     width, hidden = w_gate.shape[1:]
     top = expert_ids.shape[2]
-    place = jnp.stack([lax.axis_index("z") * experts, lax.axis_index("c")]).astype(jnp.int32)
     held = groups * SPLIT
     sent = chips * ROWS
     rows = chips * MOST
 
     swap = [(0, 1), (1, 0)]
 
-    place, down = lax.optimization_barrier((place, w_down[0]))
-    weights = jnp.concatenate([down, jnp.concatenate([w_gate[0], w_up[0]], axis=0)], axis=1)
+    weights = jnp.concatenate([w_down[0], jnp.concatenate([w_gate[0], w_up[0]], axis=0)], axis=1)
     payload = pl.pallas_call(
         functools.partial(payload_kernel, toks, width),
         out_shape=jax.ShapeDtypeStruct((SPLIT, 2 * toks * width), BF),
@@ -294,19 +291,15 @@
         functools.partial(pick_kernel, toks, experts, chips_y),
         jax.ShapeDtypeStruct((toks, sent, held), BF),
         8,
-        place,
         expert_ids[0].T,
-        smem=1,
     )
     merged = jax.ShapeDtypeStruct((toks, held, sent), BF)
     merge_hi, merge_lo, merge_pick = call(
         functools.partial(merge_kernel, toks, experts, chips_y),
         [merged, merged, merged],
         8,
-        place,
         expert_ids[0].T,
         route_weights[0].T,
-        smem=1,
     )
 
     packed = call(pack_kernel, jax.ShapeDtypeStruct((sent, 2 * width), BF), 8, pick, tokens)
@@ -318,11 +311,9 @@
         partial_kernel,
         jax.ShapeDtypeStruct((rows, 3 * hidden + 128), F32),
         20,
-        place,
         got,
         weights,
         other,
-        smem=1,
     )
     shares = partials.astype(jnp.float16).reshape(chips_y, rows // chips_y, -1)
     shares = lax.all_to_all(shares, "yl", split_axis=0, concat_axis=0, tiled=True)
@@ -338,11 +329,9 @@
         return_kernel,
         jax.ShapeDtypeStruct((sent, width + 128), BF),
         20,
-        place,
         all_grads,
         weights,
         other,
-        smem=1,
     )
     back = lax.all_to_all(
         back.reshape(chips, ROWS, -1), CHIPS, split_axis=0, concat_axis=0, tiled=True

time: 158 us -> 158 us (level)
  Pallas kernels: 9.96 us -> 7.78 us
    pallas_call x8, Pallas kernels: 9.8 us -> 7.61 us  [call(): pl.pallas_call(kernel, out_shape=out, in_specs=[pl.BlockSpec(memory_space...]
  transfers between devices with their start and end apart: 2 -> 2, of which waited for: 1 -> 1; matrix products, arithmetic and copies ran while one was open for 0% -> 0% of each run, Pallas kernels for 2% -> 1%
where the time goes in v4:
time: 158 us; the launch traced here: 157 us
  blocking collectives  126 us (80%)
  waiting for transfers between devices  10.7 us (7%)
  starting transfers between devices  9.83 us (6%)
  Pallas kernels  7.78 us (5%)
  other arithmetic  2.27 us (1%)
    all_gather x1, blocking collectives, body(): tokens = lax.all_gather(payload, 'z', axis=0, tiled=False)  43.7 us
    all_to_all x1, blocking collectives, body(): lax.all_to_all(home.reshape(groups, SPLIT, -1), 'z', split_axis=0, concat...  27.3 us
    all_to_all x1, blocking collectives, body(): lax.all_to_all(packed.reshape(chips, ROWS, 2 * width), CHIPS, split_axis=...  23.6 us
    all_to_all x1, blocking collectives, body(): lax.all_to_all(shares, 'yl', split_axis=0, concat_axis=0, tiled=True)  18 us
    all_gather x1, blocking collectives, body(): all_grads = lax.all_gather(grads, 'yl', axis=0, tiled=False)  13.3 us
    all_to_all x1, waiting for transfers between devices, body(): lax.all_to_all(back.reshape(chips, ROWS, -1), CHIPS, split_axis=0, concat...  10.7 us
    all_to_all x1, starting transfers between devices, body(): lax.all_to_all(back.reshape(chips, ROWS, -1), CHIPS, split_axis=0, concat...  7.91 us
    pallas_call x8, Pallas kernels, call(): pl.pallas_call(kernel, out_shape=out, in_specs=[pl.BlockSpec(memory_space...  7.61 us
  transfers between devices with their start and end apart: 2, of which 1 were waited for; matrix products, arithmetic and copies ran while one was open for 0% of the time, Pallas kernels for 1%

profile of v4, /device:TPU:72, one launch (start us, length us, event | category | flops | bytes accessed | tf_op | source)
XLA Modules:
  0.0 157.2 jit_solution(10116700284351289718)
XLA Ops:
  0.6 0.0 copy-start.2
  0.6 0.0 copy-start
  0.7 0.0 copy-start.1
  0.7 2.1 %maximum_maximum_fusion.own_ref = bf16[1024,1536]{1,0:T(8,128)(2,1)S(1)} fusion(bf16[512,1024]{1,0:T(8,128)(2,1)} %bitcast.29, bf16[512,1024]{1,0:T(8,128)(2,1)} %bitcast.30, bf16[1024,512]{1,0:T(8,128)(2,1)} %bitcast.31), kind=kLoop, calls=%fused_computation | loop fusion | flops 9437184 | bytes 6291456 | tf_op jit(solution)/shard_map/concatenate | solution.py:275
  2.7 1.9 %collective-permute-start = (bf16[1024,1536]{1,0:T(8,128)(2,1)S(1)}, bf16[1024,1536]{1,0:T(8,128)(2,1)S(1)}, u32[]{:S(2)}, u32[]{:S(2)}) collective-permute-start(bf16[1024,1536]{1,0:T(8,128)(2,1)S(1)} %maximum_maximum_fusion.own_ref), channel_id=1, source_target_pairs={{0,1},{1,0},{2,3},{3,2},{4,5},{5,4},{6,7},{7,6},{8,9},{9,8},{10,11... | collective-permute-start | bytes 9437192 | tf_op jit(solution)/shard_map/ppermute | solution.py:287
  4.7 0.0 copy-done.2
  4.7 0.4 shard_map.87.pick_ref
  5.1 0.0 copy-done
  5.1 0.0 copy-done.1
  5.2 0.2 shard_map.88
  5.3 43.7 %all-gather = bf16[128,3072]{1,0:T(8,128)(2,1)S(1)} all-gather(bf16[8,3072]{1,0:T(8,128)(2,1)S(1)} %shard_map.88), channel_id=2, replica_groups=mesh['z'=16,'x'=4,'yh'=2,'yl'=4,'c'=2] {'z'}, dimensions={0}, use_global_device_ids=true | all-gather | bytes 835584 | tf_op jit(solution)/shard_map/all_gather | solution.py:288
  49.0 0.6 shard_map.89
  49.6 23.6 %all_to_all.20 = bf16[32,8,1024]{2,1,0:T(8,128)(2,1)S(1)} all-to-all(bf16[32,8,1024]{2,1,0:T(8,128)(2,1)S(1)} %bitcast.22), channel_id=1, replica_groups=mesh['z'=16,'x'=4,'yh'=2,'yl'=4,'c'=2] {'x','yh','yl'}, dimensions={0} | all-to-all | bytes 1048576 | tf_op jit(solution)/shard_map/all_to_all | solution.py:306
  73.1 0.0 collective-permute-done.other_ref
  73.1 1.7 %shard_map.90 = f32[128,3200]{1,0:T(8,128)S(1)} custom-call(bf16[256,1024]{1,0:T(8,128)(2,1)S(1)} %bitcast.21, bf16[1024,1536]{1,0:T(8,128)(2,1)S(1)} %maximum_maximum_fusion.own_ref, bf16[1024,1536]{1,0:T(8,128)(2,1)S(1)} %collective-permute-done.other_ref), custom_call_target="tpu_custom_call" | custom-call | tf_op jit(solution)/shard_map/pallas_call | solution.py:35
  74.8 0.1 convert_element_type.6
  74.9 18.0 %all_to_all.21 = f16[4,32,3200]{2,1,0:T(8,128)(2,1)S(1)} all-to-all(f16[4,32,3200]{2,1,0:T(8,128)(2,1)S(1)} %bitcast.28), channel_id=1, replica_groups=mesh['z'=16,'x'=4,'yh'=2,'yl'=4,'c'=2] {'yl'}, dimensions={0} | all-to-all | bytes 1638400 | tf_op jit(solution)/shard_map/all_to_all | solution.py:319
  92.9 0.1 convert_element_type.7.p_ref
  93.0 0.3 shard_map.91
  93.3 13.3 %all-gather.1 = bf16[128,2176]{1,0:T(8,128)(2,1)S(1)} all-gather(bf16[32,2176]{1,0:T(8,128)(2,1)S(1)} %shard_map.91), channel_id=3, replica_groups=mesh['z'=16,'x'=4,'yh'=2,'yl'=4,'c'=2] {'yl'}, dimensions={0}, use_global_device_ids=true | all-gather | bytes 696320 | tf_op jit(solution)/shard_map/all_gather | solution.py:326
  106.6 0.0 copy-start.3
  106.6 2.5 %shard_map.92 = bf16[256,640]{1,0:T(8,128)(2,1)} custom-call(bf16[4,32,2176]{2,1,0:T(8,128)(2,1)S(1)} %bitcast.20, bf16[1024,1536]{1,0:T(8,128)(2,1)S(1)} %maximum_maximum_fusion.own_ref, bf16[1024,1536]{1,0:T(8,128)(2,1)S(1)} %collective-permute-done.other_ref), custom_call_target="tpu_custom_call" | custom-call | tf_op jit(solution)/shard_map/pallas_call | solution.py:35
  109.1 7.9 %all-to-all-start.2 = ((bf16[32,8,640]{2,1,0:T(8,128)(2,1)}), bf16[32,8,640]{2,1,0:T(8,128)(2,1)S(1)}, u32[]{:S(2)}, u32[]{:S(2)}) async-start(bf16[32,8,640]{2,1,0:T(8,128)(2,1)} %bitcast.13), calls=%async_computation.2 | async-start | bytes 655360 | tf_op jit(solution)/shard_map/all_to_all | solution.py:336
  117.0 0.0 copy-done.3
  117.0 1.0 shard_map.86
  117.9 10.7 %all-to-all-done.2 = bf16[32,8,640]{2,1,0:T(8,128)(2,1)S(1)} async-done(((bf16[32,8,640]{2,1,0:T(8,128)(2,1)}), bf16[32,8,640]{2,1,0:T(8,128)(2,1)S(1)}, u32[]{:S(2)}, u32[]{:S(2)}) %all-to-all-start.2) | async-done | bytes 327712 | tf_op jit(solution)/shard_map/all_to_all | solution.py:336
  128.7 0.5 shard_map.93
  129.2 27.3 %all_to_all.22.h_ref = bf16[16,8,1664]{2,1,0:T(8,128)(2,1)S(1)} all-to-all(bf16[16,8,1664]{2,1,0:T(8,128)(2,1)S(1)} %bitcast.23), channel_id=1, replica_groups=mesh['z'=16,'x'=4,'yh'=2,'yl'=4,'c'=2] {'z'}, dimensions={0} | all-to-all | bytes 851968 | tf_op jit(solution)/shard_map/all_to_all | solution.py:349
  156.5 0.7 shard_map.94
Async XLA Ops:
  0.6 4.0 %copy-start.2 = (s32[1,48,8]{1,2,0:T(8,128)S(1)}, s32[1,48,8]{1,2,0:T(8,128)}, u32[]{:S(2)}) copy-start(s32[1,48,8]{1,2,0:T(8,128)} %param.9) | copy-start | bytes 4612
  0.6 4.5 %copy-start = (bf16[1,3,4096]{2,1,0:T(4,128)(2,1)S(1)}, bf16[1,3,4096]{2,1,0:T(4,128)(2,1)}, u32[]{:S(2)}) copy-start(bf16[1,3,4096]{2,1,0:T(4,128)(2,1)} %x_hbm.1) | copy-start | bytes 73732
  0.7 4.5 %copy-start.1 = (bf16[1,3,4096]{2,1,0:T(4,128)(2,1)S(1)}, bf16[1,3,4096]{2,1,0:T(4,128)(2,1)}, u32[]{:S(2)}) copy-start(bf16[1,3,4096]{2,1,0:T(4,128)(2,1)} %g_hbm.1) | copy-start | bytes 73732
  2.7 70.4 %collective-permute-start = (bf16[1024,1536]{1,0:T(8,128)(2,1)S(1)}, bf16[1024,1536]{1,0:T(8,128)(2,1)S(1)}, u32[]{:S(2)}, u32[]{:S(2)}) collective-permute-start(bf16[1024,1536]{1,0:T(8,128)(2,1)S(1)} %maximum_maximum_fusion.own_ref), channel_id=1, source_target_pairs={{0,1},{1,0},{2,3},{3,2},{4,5},{5,4},{6,7},{7,6},{8,9},{9,8},{10,11... | collective-permute-start | bytes 9437192 | tf_op jit(solution)/shard_map/ppermute | solution.py:287
  106.6 10.4 %copy-start.3 = (f32[1,48,8]{1,2,0:T(8,128)S(1)}, f32[1,48,8]{1,2,0:T(8,128)}, u32[]{:S(2)}) copy-start(f32[1,48,8]{1,2,0:T(8,128)} %param.10) | copy-start | bytes 4612
  109.1 19.6 %all-to-all-start.2 = ((bf16[32,8,640]{2,1,0:T(8,128)(2,1)}), bf16[32,8,640]{2,1,0:T(8,128)(2,1)S(1)}, u32[]{:S(2)}, u32[]{:S(2)}) async-start(bf16[32,8,640]{2,1,0:T(8,128)(2,1)} %bitcast.13), calls=%async_computation.2 | async-start | bytes 655360 | tf_op jit(solution)/shard_map/all_to_all | solution.py:336

commit v5 on v4

--- a/solution.py
+++ b/solution.py
@@ -193,15 +193,18 @@
     a, b, r = total(0), total(1), total(2)
     sig = jax.nn.sigmoid(a)
     silu = a * sig
-    o_ref[:, :hidden] = (r * b * (sig * (1.0 + a * (1.0 - sig)))).astype(BF)
-    o_ref[:, hidden : 2 * hidden] = (r * silu).astype(BF)
+    d_gate = (r * b * (sig * (1.0 + a * (1.0 - sig)))).astype(BF)
+    d_up = (r * silu).astype(BF)
     route = jnp.sum(silu * b * r, axis=1, keepdims=True)
     hi = route.astype(BF).astype(F32)
     mid = (route - hi).astype(BF).astype(F32)
     lo = route - hi - mid
     lane = iota((route.shape[0], 128), 1)
     pieces = jnp.where(lane == 0, hi, jnp.where(lane == 1, mid, jnp.where(lane == 2, lo, 0.0)))
-    o_ref[:, 2 * hidden :] = pieces.astype(BF)
+    for j in range(o_ref.shape[0]):
+        o_ref[j, :, :hidden] = d_gate
+        o_ref[j, :, hidden : 2 * hidden] = d_up
+        o_ref[j, :, 2 * hidden :] = pieces.astype(BF)
 
 
 def return_kernel(d_ref, own_ref, other_ref, o_ref):
@@ -319,11 +322,11 @@
     shares = lax.all_to_all(shares, "yl", split_axis=0, concat_axis=0, tiled=True)
     grads = call(
         functools.partial(hidden_kernel, hidden),
-        jax.ShapeDtypeStruct((rows // chips_y, 2 * hidden + 128), BF),
+        jax.ShapeDtypeStruct((chips_y, rows // chips_y, 2 * hidden + 128), BF),
         8,
         shares.astype(F32),
     )
-    all_grads = lax.all_gather(grads, "yl", axis=0, tiled=False)
+    all_grads = lax.all_to_all(grads, "yl", split_axis=0, concat_axis=0, tiled=True)
 
     back = call(
         return_kernel,

time: 158 us -> 156 us (0.987)
    all_gather x1 -> x0, blocking collectives: 13.3 us -> none  [body(): all_grads = lax.all_gather(grads, 'yl', axis=0, tiled=False)]
    all_to_all x0 -> x1, blocking collectives: none -> 13.2 us  [body(): lax.all_to_all(grads, 'yl', split_axis=0, concat_axis=0, tiled=True)]
    all_to_all x1, blocking collectives: 18 us -> 15.7 us  [body(): lax.all_to_all(shares, 'yl', split_axis=0, concat_axis=0, tiled=True)]
    all_to_all x1, blocking collectives: 27.3 us -> 29.5 us  [body(): lax.all_to_all(home.reshape(groups, SPLIT, -1), 'z', split_axis=0, concat...]
where the time goes in v5:
time: 156 us; the launch traced here: 155 us
  blocking collectives  126 us (81%)
  waiting for transfers between devices  10.7 us (7%)
  starting transfers between devices  8.26 us (5%)
  Pallas kernels  7.78 us (5%)
  other arithmetic  2.27 us (1%)
    all_gather x1, blocking collectives, body(): tokens = lax.all_gather(payload, 'z', axis=0, tiled=False)  43.7 us
    all_to_all x1, blocking collectives, body(): lax.all_to_all(home.reshape(groups, SPLIT, -1), 'z', split_axis=0, concat...  29.5 us
    all_to_all x1, blocking collectives, body(): lax.all_to_all(packed.reshape(chips, ROWS, 2 * width), CHIPS, split_axis=...  23.6 us
    all_to_all x1, blocking collectives, body(): lax.all_to_all(shares, 'yl', split_axis=0, concat_axis=0, tiled=True)  15.7 us
    all_to_all x1, blocking collectives, body(): lax.all_to_all(grads, 'yl', split_axis=0, concat_axis=0, tiled=True)  13.2 us
    all_to_all x1, waiting for transfers between devices, body(): lax.all_to_all(back.reshape(chips, ROWS, -1), CHIPS, split_axis=0, concat...  10.7 us
    pallas_call x8, Pallas kernels, call(): pl.pallas_call(kernel, out_shape=out, in_specs=[pl.BlockSpec(memory_space...  7.61 us
    all_to_all x1, starting transfers between devices, body(): lax.all_to_all(back.reshape(chips, ROWS, -1), CHIPS, split_axis=0, concat...  6.34 us
  transfers between devices with their start and end apart: 2, of which 1 were waited for; matrix products, arithmetic and copies ran while one was open for 0% of the time, Pallas kernels for 1%

profile of v5, /device:TPU:72, one launch (start us, length us, event | category | flops | bytes accessed | tf_op | source)
XLA Modules:
  0.0 155.5 jit_solution(17746281507156467206)
XLA Ops:
  0.6 0.0 copy-start.2
  0.6 0.0 copy-start
  0.7 0.0 copy-start.1
  0.7 2.1 %maximum_maximum_fusion.own_ref = bf16[1024,1536]{1,0:T(8,128)(2,1)S(1)} fusion(bf16[512,1024]{1,0:T(8,128)(2,1)} %bitcast.27, bf16[512,1024]{1,0:T(8,128)(2,1)} %bitcast.28, bf16[1024,512]{1,0:T(8,128)(2,1)} %bitcast.29), kind=kLoop, calls=%fused_computation | loop fusion | flops 9437184 | bytes 6291456 | tf_op jit(solution)/shard_map/concatenate | solution.py:278
  2.7 1.9 %collective-permute-start = (bf16[1024,1536]{1,0:T(8,128)(2,1)S(1)}, bf16[1024,1536]{1,0:T(8,128)(2,1)S(1)}, u32[]{:S(2)}, u32[]{:S(2)}) collective-permute-start(bf16[1024,1536]{1,0:T(8,128)(2,1)S(1)} %maximum_maximum_fusion.own_ref), channel_id=1, source_target_pairs={{0,1},{1,0},{2,3},{3,2},{4,5},{5,4},{6,7},{7,6},{8,9},{9,8},{10,11... | collective-permute-start | bytes 9437192 | tf_op jit(solution)/shard_map/ppermute | solution.py:290
  4.7 0.0 copy-done.2
  4.7 0.4 shard_map.87.pick_ref
  5.1 0.0 copy-done
  5.1 0.0 copy-done.1
  5.2 0.2 shard_map.88
  5.3 43.7 %all-gather = bf16[128,3072]{1,0:T(8,128)(2,1)S(1)} all-gather(bf16[8,3072]{1,0:T(8,128)(2,1)S(1)} %shard_map.88), channel_id=2, replica_groups=mesh['z'=16,'x'=4,'yh'=2,'yl'=4,'c'=2] {'z'}, dimensions={0}, use_global_device_ids=true | all-gather | bytes 835584 | tf_op jit(solution)/shard_map/all_gather | solution.py:291
  49.0 0.6 shard_map.89
  49.6 23.6 %all_to_all.25 = bf16[32,8,1024]{2,1,0:T(8,128)(2,1)S(1)} all-to-all(bf16[32,8,1024]{2,1,0:T(8,128)(2,1)S(1)} %bitcast.20), channel_id=1, replica_groups=mesh['z'=16,'x'=4,'yh'=2,'yl'=4,'c'=2] {'x','yh','yl'}, dimensions={0} | all-to-all | bytes 1048576 | tf_op jit(solution)/shard_map/all_to_all | solution.py:309
  73.1 0.0 collective-permute-done.other_ref
  73.1 1.7 %shard_map.90 = f32[128,3200]{1,0:T(8,128)S(1)} custom-call(bf16[256,1024]{1,0:T(8,128)(2,1)S(1)} %bitcast.19, bf16[1024,1536]{1,0:T(8,128)(2,1)S(1)} %maximum_maximum_fusion.own_ref, bf16[1024,1536]{1,0:T(8,128)(2,1)S(1)} %collective-permute-done.other_ref), custom_call_target="tpu_custom_call" | custom-call | tf_op jit(solution)/shard_map/pallas_call | solution.py:35
  74.8 0.1 convert_element_type.6
  74.9 15.7 %all_to_all.26 = f16[4,32,3200]{2,1,0:T(8,128)(2,1)S(1)} all-to-all(f16[4,32,3200]{2,1,0:T(8,128)(2,1)S(1)} %bitcast.26), channel_id=1, replica_groups=mesh['z'=16,'x'=4,'yh'=2,'yl'=4,'c'=2] {'yl'}, dimensions={0} | all-to-all | bytes 1638400 | tf_op jit(solution)/shard_map/all_to_all | solution.py:322
  90.6 0.1 convert_element_type.7.p_ref
  90.8 0.3 shard_map.91
  91.1 13.2 %all_to_all.27.d_ref = bf16[4,32,2176]{2,1,0:T(8,128)(2,1)S(1)} all-to-all(bf16[4,32,2176]{2,1,0:T(8,128)(2,1)S(1)} %shard_map.91), channel_id=1, replica_groups=mesh['z'=16,'x'=4,'yh'=2,'yl'=4,'c'=2] {'yl'}, dimensions={0} | all-to-all | bytes 1114112 | tf_op jit(solution)/shard_map/all_to_all | solution.py:329
  104.2 0.0 copy-start.3
  104.2 2.5 %shard_map.92 = bf16[256,640]{1,0:T(8,128)(2,1)} custom-call(bf16[4,32,2176]{2,1,0:T(8,128)(2,1)S(1)} %all_to_all.27.d_ref, bf16[1024,1536]{1,0:T(8,128)(2,1)S(1)} %maximum_maximum_fusion.own_ref, bf16[1024,1536]{1,0:T(8,128)(2,1)S(1)} %collective-permute-done.other_ref), custom_call_target="tpu_custom_call" | custom-call | tf_op jit(solution)/shard_map/pallas_call | solution.py:35
  106.7 6.3 %all-to-all-start.3 = ((bf16[32,8,640]{2,1,0:T(8,128)(2,1)}), bf16[32,8,640]{2,1,0:T(8,128)(2,1)S(1)}, u32[]{:S(2)}, u32[]{:S(2)}) async-start(bf16[32,8,640]{2,1,0:T(8,128)(2,1)} %bitcast.12), calls=%async_computation.3 | async-start | bytes 655360 | tf_op jit(solution)/shard_map/all_to_all | solution.py:339
  113.1 0.0 copy-done.3
  113.1 1.0 shard_map.86
  114.1 10.7 %all-to-all-done.3 = bf16[32,8,640]{2,1,0:T(8,128)(2,1)S(1)} async-done(((bf16[32,8,640]{2,1,0:T(8,128)(2,1)}), bf16[32,8,640]{2,1,0:T(8,128)(2,1)S(1)}, u32[]{:S(2)}, u32[]{:S(2)}) %all-to-all-start.3) | async-done | bytes 327712 | tf_op jit(solution)/shard_map/all_to_all | solution.py:339
  124.8 0.5 shard_map.93
  125.3 29.5 %all_to_all.28.h_ref = bf16[16,8,1664]{2,1,0:T(8,128)(2,1)S(1)} all-to-all(bf16[16,8,1664]{2,1,0:T(8,128)(2,1)S(1)} %bitcast.21), channel_id=1, replica_groups=mesh['z'=16,'x'=4,'yh'=2,'yl'=4,'c'=2] {'z'}, dimensions={0} | all-to-all | bytes 851968 | tf_op jit(solution)/shard_map/all_to_all | solution.py:352
  154.8 0.7 shard_map.94
Async XLA Ops:
  0.6 4.0 %copy-start.2 = (s32[1,48,8]{1,2,0:T(8,128)S(1)}, s32[1,48,8]{1,2,0:T(8,128)}, u32[]{:S(2)}) copy-start(s32[1,48,8]{1,2,0:T(8,128)} %param.9) | copy-start | bytes 4612
  0.6 4.5 %copy-start = (bf16[1,3,4096]{2,1,0:T(4,128)(2,1)S(1)}, bf16[1,3,4096]{2,1,0:T(4,128)(2,1)}, u32[]{:S(2)}) copy-start(bf16[1,3,4096]{2,1,0:T(4,128)(2,1)} %x_hbm.1) | copy-start | bytes 73732
  0.7 4.5 %copy-start.1 = (bf16[1,3,4096]{2,1,0:T(4,128)(2,1)S(1)}, bf16[1,3,4096]{2,1,0:T(4,128)(2,1)}, u32[]{:S(2)}) copy-start(bf16[1,3,4096]{2,1,0:T(4,128)(2,1)} %g_hbm.1) | copy-start | bytes 73732
  2.7 70.4 %collective-permute-start = (bf16[1024,1536]{1,0:T(8,128)(2,1)S(1)}, bf16[1024,1536]{1,0:T(8,128)(2,1)S(1)}, u32[]{:S(2)}, u32[]{:S(2)}) collective-permute-start(bf16[1024,1536]{1,0:T(8,128)(2,1)S(1)} %maximum_maximum_fusion.own_ref), channel_id=1, source_target_pairs={{0,1},{1,0},{2,3},{3,2},{4,5},{5,4},{6,7},{7,6},{8,9},{9,8},{10,11... | collective-permute-start | bytes 9437192 | tf_op jit(solution)/shard_map/ppermute | solution.py:290
  104.2 8.8 %copy-start.3 = (f32[1,48,8]{1,2,0:T(8,128)S(1)}, f32[1,48,8]{1,2,0:T(8,128)}, u32[]{:S(2)}) copy-start(f32[1,48,8]{1,2,0:T(8,128)} %param.10) | copy-start | bytes 4612
  106.7 18.0 %all-to-all-start.3 = ((bf16[32,8,640]{2,1,0:T(8,128)(2,1)}), bf16[32,8,640]{2,1,0:T(8,128)(2,1)S(1)}, u32[]{:S(2)}, u32[]{:S(2)}) async-start(bf16[32,8,640]{2,1,0:T(8,128)(2,1)} %bitcast.12), calls=%async_computation.3 | async-start | bytes 655360 | tf_op jit(solution)/shard_map/all_to_all | solution.py:339

commit v6 on v5

--- a/solution.py
+++ b/solution.py
@@ -305,6 +305,7 @@
         route_weights[0].T,
     )
 
+    tokens, merge_hi = lax.optimization_barrier((tokens, merge_hi))
     packed = call(pack_kernel, jax.ShapeDtypeStruct((sent, 2 * width), BF), 8, pick, tokens)
     got = lax.all_to_all(
         packed.reshape(chips, ROWS, 2 * width), CHIPS, split_axis=0, concat_axis=0, tiled=True

time: 156 us -> 158 us (1.013)
  blocking collectives: 126 us -> 145 us
  waiting for transfers between devices: 10.7 us -> 0.01 us
  starting transfers between devices: 8.26 us -> 1.92 us
    all_to_all x0 -> x1, blocking collectives: none -> 17.8 us  [body(): lax.all_to_all(back.reshape(chips, ROWS, -1), CHIPS, split_axis=0, concat...]
    all_to_all x1 -> x0, waiting for transfers between devices: 10.7 us -> none  [body(): lax.all_to_all(back.reshape(chips, ROWS, -1), CHIPS, split_axis=0, concat...]
    all_to_all x1 -> x0, starting transfers between devices: 6.34 us -> none  [body(): lax.all_to_all(back.reshape(chips, ROWS, -1), CHIPS, split_axis=0, concat...]
    all_to_all x1, blocking collectives: 29.5 us -> 31.2 us  [body(): lax.all_to_all(home.reshape(groups, SPLIT, -1), 'z', split_axis=0, concat...]
  transfers between devices with their start and end apart: 2 -> 1, of which waited for: 1 -> 0; matrix products, arithmetic and copies ran while one was open for 0% -> 0% of each run, Pallas kernels for 1% -> 1%
where the time goes in v6:
time: 158 us; the launch traced here: 157 us
  blocking collectives  145 us (92%)
  Pallas kernels  7.05 us (4%)
  other arithmetic  2.27 us (1%)
  starting transfers between devices  1.92 us (1%)
    all_gather x1, blocking collectives, body(): tokens = lax.all_gather(payload, 'z', axis=0, tiled=False)  43.7 us
    all_to_all x1, blocking collectives, body(): lax.all_to_all(home.reshape(groups, SPLIT, -1), 'z', split_axis=0, concat...  31.2 us
    all_to_all x1, blocking collectives, body(): lax.all_to_all(packed.reshape(chips, ROWS, 2 * width), CHIPS, split_axis=...  23.6 us
    all_to_all x1, blocking collectives, body(): lax.all_to_all(back.reshape(chips, ROWS, -1), CHIPS, split_axis=0, concat...  17.8 us
    all_to_all x1, blocking collectives, body(): lax.all_to_all(shares, 'yl', split_axis=0, concat_axis=0, tiled=True)  15.8 us
    all_to_all x1, blocking collectives, body(): lax.all_to_all(grads, 'yl', split_axis=0, concat_axis=0, tiled=True)  13.2 us
    pallas_call x8, Pallas kernels, call(): pl.pallas_call(kernel, out_shape=out, in_specs=[pl.BlockSpec(memory_space...  6.89 us
  transfers between devices with their start and end apart: 1, of which 0 were waited for; matrix products, arithmetic and copies ran while one was open for 0% of the time, Pallas kernels for 1%

profile of v6, /device:TPU:72, one launch (start us, length us, event | category | flops | bytes accessed | tf_op | source)
XLA Modules:
  0.0 157.3 jit_solution(7261732651634714068)
XLA Ops:
  0.6 0.0 copy-start.2
  0.6 0.0 copy-start.3
  0.7 0.0 copy-start
  0.7 0.0 copy-start.1
  0.7 2.1 %maximum_maximum_fusion.own_ref = bf16[1024,1536]{1,0:T(8,128)(2,1)S(1)} fusion(bf16[512,1024]{1,0:T(8,128)(2,1)} %bitcast.28, bf16[512,1024]{1,0:T(8,128)(2,1)} %bitcast.29, bf16[1024,512]{1,0:T(8,128)(2,1)} %bitcast.30), kind=kLoop, calls=%fused_computation | loop fusion | flops 9437184 | bytes 6291456 | tf_op jit(solution)/shard_map/concatenate | solution.py:278
  2.8 1.9 %collective-permute-start = (bf16[1024,1536]{1,0:T(8,128)(2,1)S(1)}, bf16[1024,1536]{1,0:T(8,128)(2,1)S(1)}, u32[]{:S(2)}, u32[]{:S(2)}) collective-permute-start(bf16[1024,1536]{1,0:T(8,128)(2,1)S(1)} %maximum_maximum_fusion.own_ref), channel_id=1, source_target_pairs={{0,1},{1,0},{2,3},{3,2},{4,5},{5,4},{6,7},{7,6},{8,9},{9,8},{10,11... | collective-permute-start | bytes 9437192 | tf_op jit(solution)/shard_map/ppermute | solution.py:290
  4.7 0.0 copy-done.2
  4.7 0.4 shard_map.88.pick_ref
  5.1 0.0 copy-done.3
  5.2 1.0 shard_map.87
  6.1 0.0 copy-done
  6.1 0.0 copy-done.1
  6.1 0.2 shard_map.86
  6.3 43.7 %all-gather = bf16[128,3072]{1,0:T(8,128)(2,1)S(1)} all-gather(bf16[8,3072]{1,0:T(8,128)(2,1)S(1)} %shard_map.86), channel_id=2, replica_groups=mesh['z'=16,'x'=4,'yh'=2,'yl'=4,'c'=2] {'z'}, dimensions={0}, use_global_device_ids=true | all-gather | bytes 835584 | tf_op jit(solution)/shard_map/all_gather | solution.py:291
  50.0 0.6 shard_map.89
  50.5 23.6 %all_to_all.25 = bf16[32,8,1024]{2,1,0:T(8,128)(2,1)S(1)} all-to-all(bf16[32,8,1024]{2,1,0:T(8,128)(2,1)S(1)} %bitcast.20), channel_id=1, replica_groups=mesh['z'=16,'x'=4,'yh'=2,'yl'=4,'c'=2] {'x','yh','yl'}, dimensions={0} | all-to-all | bytes 1048576 | tf_op jit(solution)/shard_map/all_to_all | solution.py:310
  74.1 0.0 collective-permute-done.other_ref
  74.1 1.7 %shard_map.90 = f32[128,3200]{1,0:T(8,128)S(1)} custom-call(bf16[256,1024]{1,0:T(8,128)(2,1)S(1)} %bitcast.19, bf16[1024,1536]{1,0:T(8,128)(2,1)S(1)} %maximum_maximum_fusion.own_ref, bf16[1024,1536]{1,0:T(8,128)(2,1)S(1)} %collective-permute-done.other_ref), custom_call_target="tpu_custom_call" | custom-call | tf_op jit(solution)/shard_map/pallas_call | solution.py:35
  75.8 0.1 convert_element_type.6
  75.9 15.8 %all_to_all.26 = f16[4,32,3200]{2,1,0:T(8,128)(2,1)S(1)} all-to-all(f16[4,32,3200]{2,1,0:T(8,128)(2,1)S(1)} %bitcast.27), channel_id=1, replica_groups=mesh['z'=16,'x'=4,'yh'=2,'yl'=4,'c'=2] {'yl'}, dimensions={0} | all-to-all | bytes 1638400 | tf_op jit(solution)/shard_map/all_to_all | solution.py:323
  91.6 0.1 convert_element_type.7.p_ref
  91.8 0.3 shard_map.91
  92.1 13.2 %all_to_all.27.d_ref = bf16[4,32,2176]{2,1,0:T(8,128)(2,1)S(1)} all-to-all(bf16[4,32,2176]{2,1,0:T(8,128)(2,1)S(1)} %shard_map.91), channel_id=1, replica_groups=mesh['z'=16,'x'=4,'yh'=2,'yl'=4,'c'=2] {'yl'}, dimensions={0} | all-to-all | bytes 1114112 | tf_op jit(solution)/shard_map/all_to_all | solution.py:330
  105.2 1.8 %shard_map.92 = bf16[256,640]{1,0:T(8,128)(2,1)S(1)} custom-call(bf16[4,32,2176]{2,1,0:T(8,128)(2,1)S(1)} %all_to_all.27.d_ref, bf16[1024,1536]{1,0:T(8,128)(2,1)S(1)} %maximum_maximum_fusion.own_ref, bf16[1024,1536]{1,0:T(8,128)(2,1)S(1)} %collective-permute-done.other_ref), custom_call_target="tpu_custom_call" | custom-call | tf_op jit(solution)/shard_map/pallas_call | solution.py:35
  107.0 17.8 %all_to_all.28 = bf16[32,8,640]{2,1,0:T(8,128)(2,1)S(1)} all-to-all(bf16[32,8,640]{2,1,0:T(8,128)(2,1)S(1)} %bitcast.22), channel_id=1, replica_groups=mesh['z'=16,'x'=4,'yh'=2,'yl'=4,'c'=2] {'x','yh','yl'}, dimensions={0} | all-to-all | bytes 655360 | tf_op jit(solution)/shard_map/all_to_all | solution.py:340
  124.8 0.5 shard_map.93
  125.4 31.2 %all_to_all.29.h_ref = bf16[16,8,1664]{2,1,0:T(8,128)(2,1)S(1)} all-to-all(bf16[16,8,1664]{2,1,0:T(8,128)(2,1)S(1)} %bitcast.21), channel_id=1, replica_groups=mesh['z'=16,'x'=4,'yh'=2,'yl'=4,'c'=2] {'z'}, dimensions={0} | all-to-all | bytes 851968 | tf_op jit(solution)/shard_map/all_to_all | solution.py:353
  156.6 0.7 shard_map.94
Async XLA Ops:
  0.6 4.1 %copy-start.2 = (s32[1,48,8]{1,2,0:T(8,128)S(1)}, s32[1,48,8]{1,2,0:T(8,128)}, u32[]{:S(2)}) copy-start(s32[1,48,8]{1,2,0:T(8,128)} %param.9) | copy-start | bytes 4612
  0.6 4.5 %copy-start.3 = (f32[1,48,8]{1,2,0:T(8,128)S(1)}, f32[1,48,8]{1,2,0:T(8,128)}, u32[]{:S(2)}) copy-start(f32[1,48,8]{1,2,0:T(8,128)} %param.10) | copy-start | bytes 4612
  0.7 5.5 %copy-start = (bf16[1,3,4096]{2,1,0:T(4,128)(2,1)S(1)}, bf16[1,3,4096]{2,1,0:T(4,128)(2,1)}, u32[]{:S(2)}) copy-start(bf16[1,3,4096]{2,1,0:T(4,128)(2,1)} %x_hbm.1) | copy-start | bytes 73732
  0.7 5.5 %copy-start.1 = (bf16[1,3,4096]{2,1,0:T(4,128)(2,1)S(1)}, bf16[1,3,4096]{2,1,0:T(4,128)(2,1)}, u32[]{:S(2)}) copy-start(bf16[1,3,4096]{2,1,0:T(4,128)(2,1)} %g_hbm.1) | copy-start | bytes 73732
  2.8 71.4 %collective-permute-start = (bf16[1024,1536]{1,0:T(8,128)(2,1)S(1)}, bf16[1024,1536]{1,0:T(8,128)(2,1)S(1)}, u32[]{:S(2)}, u32[]{:S(2)}) collective-permute-start(bf16[1024,1536]{1,0:T(8,128)(2,1)S(1)} %maximum_maximum_fusion.own_ref), channel_id=1, source_target_pairs={{0,1},{1,0},{2,3},{3,2},{4,5},{5,4},{6,7},{7,6},{8,9},{9,8},{10,11... | collective-permute-start | bytes 9437192 | tf_op jit(solution)/shard_map/ppermute | solution.py:290
